TPU v7x, 512 devices: a whole 4x4x16 slice. The times are simulated.
512 devices in a mesh: gx: 4 (over y), gy: 8 (over x, core), gz: 16 (over z).
Axes of the slice: x: 4, y: 4, z: 16, core: 2. Of those that a mesh axis runs over, the one named last changes fastest.
Arguments:
- a_blocks: bfloat16 [4, 16, 32, 7, 128, 128], P('gx', 'gy', 'gz'), may hold values from -0.25 to 2
- a_cols: int32 [4, 16, 32, 7], P('gx', 'gy', 'gz'), may hold values from 0 to 2047, as said below
- p_blocks: bfloat16 [4, 16, 32, 128, 128], P('gx', 'gy', 'gz'), may hold values from -0.05 to 1.7
- agg_ids: int32 [4, 16, 32], P('gx', 'gy', 'gz'), may hold values from 0 to 1023, as said below
- coarse_cols: int32 [4, 16, 16, 11], P('gx', 'gy', 'gz'), may hold values from 0 to 1023, as said below
- coarse_rhs: float32 [4, 16, 16, 128], P('gx', 'gy', 'gz'), may hold values from -6 to 6
- coarse_start: float32 [4, 16, 16, 128], P('gx', 'gy', 'gz'), may hold values from -6 to 6
Outputs:
- coarse_solution: float32 [4, 16, 16, 128], P('gx', 'gy', 'gz')
- coarse_residual: float32 [4, 16, 16, 128], P('gx', 'gy', 'gz')
Inputs may be any that keep to these rules, and one draw needn't show every extreme that they name: `a_cols`: entry [x, y, z, :] lists, in some order, the flat id of tile (x, y, z) itself and of its six face neighbours, indices taken modulo 4, 16 and 32. `agg_ids`: each column (x, y) has a phase s of 0 or 1; tile (x, y, z) belongs to aggregate (x * 16 + y) * 16 + k with k = ((z - s) mod 32) // 2, so aggregate k holds the tiles 2 k + s and 2 k + s + 1 (mod 32) of its column. `coarse_cols`: row (x, y, k) lists in slots 0, 1, 2 the aggregates k - 1, k, k + 1 (mod 16) of its own column, and in slot 3 + 2 d + j the aggregate holding the neighbour, in direction d (-x, +x, -y, +y, periodic), of its member tile j (0 the lower, 1 the upper).
All inputs are finite; a program needn't handle non-finite values.
Results may differ from a plain program's by a relative error of at most 0.00046.
Values may be sent and summed in bfloat16 or wider, within the bound.
A program may use at most 64 MiB of HBM per device.

v0:
```python
import jax
import jax.numpy as jnp
from jax import lax
from jax.sharding import PartitionSpec as P

EPSILON = 1e-05


def extended(block, sides, width):
    for axis, dim in sides:
        count = lax.axis_size(axis)
        forward = [(i, i + 1) for i in range(count - 1)]
        forward.append((count - 1, 0))
        backward = [(target, source) for source, target in forward]
        low = lax.ppermute(
            lax.slice_in_dim(block, block.shape[dim] - width, None, axis=dim), axis, forward
        )
        high = lax.ppermute(lax.slice_in_dim(block, 0, width, axis=dim), axis, backward)
        block = jnp.concatenate([low, block, high], axis=dim)
    return block


def shifted(block, axis, distance):
    devices = range(lax.axis_size(axis))
    route = [((i - distance) % len(devices), i) for i in devices]
    return lax.ppermute(block, axis, route)


def direction_code(off_x, off_y, off_z):
    inner = jnp.where(off_y == -1, 5, jnp.where(off_y == 1, 6, 0))
    inner = jnp.where(off_x == -1, 3, jnp.where(off_x == 1, 4, inner))
    return jnp.where(off_z == -1, 1, jnp.where(off_z == 1, 2, inner)).astype(jnp.int32)


def slot_of(direction, member):
    return jnp.where(
        direction == 0,
        1,
        jnp.where(
            direction == 1,
            member,
            jnp.where(direction == 2, 1 + member, 2 * direction - 3 + member),
        ),
    )


def wrapped(target, anchor, length):
    return (target - anchor + 1) % length - 1


def coarse_halo(values):
    return extended(values, (("gx", 0), ("gy", 1), ("gz", 2)), 1)


def apply_coarse(operator, padded, index_flat):
    width = padded.shape[-1]
    picked = padded.reshape(-1, width)[index_flat]
    return jnp.einsum("abcsij,abcsj->abci", operator, picked, precision=lax.Precision.HIGHEST)


def body(a_blocks, a_cols, p_blocks, agg_ids, coarse_cols, coarse_rhs, coarse_start):
    tiles_x, tiles_y, tiles_z = (p_blocks.shape[0], p_blocks.shape[1], p_blocks.shape[2])
    blocks = p_blocks.shape[3]
    entries = a_cols.shape[3]
    slots = coarse_cols.shape[3]
    layers = tiles_z // 2
    total_x = tiles_x * lax.axis_size("gx")
    total_y = tiles_y * lax.axis_size("gy")
    total_z = tiles_z * lax.axis_size("gz")
    half_z = total_z // 2
    start_x = lax.axis_index("gx") * tiles_x
    start_y = lax.axis_index("gy") * tiles_y
    start_z = lax.axis_index("gz") * tiles_z
    start_layer = lax.axis_index("gz") * layers
    own_x = start_x + jnp.arange(tiles_x, dtype=jnp.int32)[:, None, None]
    own_y = start_y + jnp.arange(tiles_y, dtype=jnp.int32)[None, :, None]
    own_z = start_z + jnp.arange(tiles_z, dtype=jnp.int32)[None, None, :]
    local_x = jnp.arange(tiles_x, dtype=jnp.int32)[:, None, None, None]
    local_y = jnp.arange(tiles_y, dtype=jnp.int32)[None, :, None, None]
    local_z = jnp.arange(tiles_z, dtype=jnp.int32)[None, None, :, None]
    padded_p = extended(p_blocks, (("gx", 0), ("gy", 1), ("gz", 2)), 1)
    off_x = wrapped(a_cols // (total_y * total_z), own_x[..., None], total_x)
    off_y = wrapped(a_cols // total_z % total_y, own_y[..., None], total_y)
    off_z = wrapped(a_cols % total_z, own_z[..., None], total_z)
    index_flat = ((local_x + 1 + off_x) * (tiles_y + 2) + (local_y + 1 + off_y)) * (tiles_z + 2) + (
        local_z + 1 + off_z
    )
    gathered = padded_p.reshape(-1, blocks, blocks)[index_flat]
    products = jnp.einsum(
        "abcenm,abceml->abcenl", a_blocks, gathered, preferred_element_type=jnp.float32
    ).astype(jnp.bfloat16)
    pieces = jnp.einsum(
        "abcmn,abceml->abcenl", p_blocks, products, preferred_element_type=jnp.float32
    )
    direction = direction_code(off_x, off_y, off_z)
    layer = agg_ids % half_z
    phase = (start_layer - layer[:, :, 0]) % half_z
    member = (own_z - phase[:, :, None]) % 2
    slot_index = slot_of(direction, member[..., None])
    local_layer = (layer - start_layer) % half_z
    owned = local_layer < layers
    target = local_layer[..., None] * slots + slot_index
    onehot = (
        (target[..., None] == jnp.arange(layers * slots, dtype=jnp.int32)) & owned[..., None, None]
    ).astype(jnp.float32)
    onehot = onehot.reshape(tiles_x, tiles_y, tiles_z * entries, layers * slots)
    summed = jnp.einsum(
        "abeq,abex->abqx",
        onehot,
        pieces.reshape(tiles_x, tiles_y, tiles_z * entries, blocks * blocks),
        precision=lax.Precision.HIGHEST,
    )
    lowest = direction[:, :, 0, :]
    straddle = (phase == 1).astype(jnp.float32)
    upper_slot = slot_of(jnp.arange(entries, dtype=jnp.int32), 1)
    upper_hot = (upper_slot[:, None] == jnp.arange(slots, dtype=jnp.int32)[None, :]).astype(
        jnp.float32
    )
    order = jnp.sum(
        jnp.arange(entries, dtype=jnp.int32)[None, None, None, :]
        * (lowest[:, :, None, :] == jnp.arange(entries, dtype=jnp.int32)[None, None, :, None]),
        axis=-1,
    )
    row_x = jnp.arange(tiles_x, dtype=jnp.int32)[:, None, None]
    row_y = jnp.arange(tiles_y, dtype=jnp.int32)[None, :, None]
    arrived = shifted(pieces[:, :, 0][row_x, row_y, order], "gz", -1)
    extra = (
        jnp.einsum(
            "eq,abex->abqx",
            upper_hot,
            arrived.reshape(tiles_x, tiles_y, entries, blocks * blocks),
            precision=lax.Precision.HIGHEST,
        )
        * straddle[:, :, None, None]
    )
    operator = summed.reshape(tiles_x, tiles_y, layers, slots, blocks * blocks)
    operator = operator.at[:, :, layers - 1].add(extra)
    operator = operator.reshape(tiles_x, tiles_y, layers, slots, blocks, blocks)
    scale = jnp.sum(jnp.abs(operator), axis=(3, 5)) + EPSILON
    own_k = start_layer + jnp.arange(layers, dtype=jnp.int32)[None, None, :, None]
    local_k = jnp.arange(layers, dtype=jnp.int32)[None, None, :, None]
    coarse_x = wrapped(coarse_cols // (total_y * half_z), own_x[..., None], total_x)
    coarse_y = wrapped(coarse_cols // half_z % total_y, own_y[..., None], total_y)
    coarse_k = wrapped(coarse_cols % half_z, own_k, half_z)
    coarse_index = ((local_x + 1 + coarse_x) * (tiles_y + 2) + (local_y + 1 + coarse_y)) * (
        layers + 2
    ) + (local_k + 1 + coarse_k)
    start_padded = coarse_halo(coarse_start)
    middle = (
        coarse_start + (coarse_rhs - apply_coarse(operator, start_padded, coarse_index)) / scale
    )
    solution = (
        middle + (coarse_rhs - apply_coarse(operator, coarse_halo(middle), coarse_index)) / scale
    )
    residual = coarse_rhs - apply_coarse(operator, coarse_halo(solution), coarse_index)
    return (solution, residual)


def solution(mesh):
    return jax.shard_map(
        body,
        mesh=mesh,
        in_specs=(
            P("gx", "gy", "gz", None, None, None),
            P("gx", "gy", "gz", None),
            P("gx", "gy", "gz", None, None),
            P("gx", "gy", "gz"),
            P("gx", "gy", "gz", None),
            P("gx", "gy", "gz", None),
            P("gx", "gy", "gz", None),
        ),
        out_specs=(P("gx", "gy", "gz", None), P("gx", "gy", "gz", None)),
        check_vma=False,
    )
```

profile of v0, /device:TPU:1, one launch (start us, length us, event | category | flops | bytes accessed | tf_op | source)
XLA Modules:
  0.0 156.5 jit_solution(8671604215826416716)
XLA Ops:
  0.6 5.6 %collective-permute-start.8 = (f32[1,2,1,128]{3,2,1,0:T(1,128)}, f32[1,2,1,128]{3,2,1,0:T(1,128)S(1)}, u32[]{:S(2)}, u32[]{:S(2)}) collective-permute-start(f32[1,2,1,128]{3,2,1,0:T(1,128)} %param.15), channel_id=1, source_target_pairs={{128,0},{256,128},{384,256},{0,384},{129,1},{257,129},{385,257},{1... | collective-permute-start | bytes 3080 | tf_op jit(solution)/shard_map/ppermute | solution.py:18
  6.3 1.9 %collective-permute-start.7 = (f32[1,2,1,128]{3,2,1,0:T(1,128)}, f32[1,2,1,128]{3,2,1,0:T(1,128)S(1)}, u32[]{:S(2)}, u32[]{:S(2)}) collective-permute-start(f32[1,2,1,128]{3,2,1,0:T(1,128)} %param.15), channel_id=1, source_target_pairs={{0,128},{128,256},{256,384},{384,0},{1,129},{129,257},{257,385},{3... | collective-permute-start | bytes 3080 | tf_op jit(solution)/shard_map/ppermute | solution.py:15
  8.2 4.6 %collective-permute-start.1 = (bf16[1,2,2,128,128]{4,3,2,1,0:T(8,128)(2,1)}, bf16[1,2,2,128,128]{4,3,2,1,0:T(8,128)(2,1)S(1)}, u32[]{:S(2)}, u32[]{:S(2)}) collective-permute-start(bf16[1,2,2,128,128]{4,3,2,1,0:T(8,128)(2,1)} %param.11), channel_id=1, source_target_pairs={{128,0},{256,128},{384,256},{0,384},{129,1},{257,129},{385,257},{1... | collective-permute-start | bytes 393224 | tf_op jit(solution)/shard_map/ppermute | solution.py:18
  12.8 1.9 %collective-permute-start = (bf16[1,2,2,128,128]{4,3,2,1,0:T(8,128)(2,1)}, bf16[1,2,2,128,128]{4,3,2,1,0:T(8,128)(2,1)S(1)}, u32[]{:S(2)}, u32[]{:S(2)}) collective-permute-start(bf16[1,2,2,128,128]{4,3,2,1,0:T(8,128)(2,1)} %param.11), channel_id=1, source_target_pairs={{0,128},{128,256},{256,384},{384,0},{1,129},{129,257},{257,385},{3... | collective-permute-start | bytes 393224 | tf_op jit(solution)/shard_map/ppermute | solution.py:15
  17.7 2.2 %collective-permute-done = bf16[1,2,2,128,128]{4,3,2,1,0:T(8,128)(2,1)S(1)} collective-permute-done((bf16[1,2,2,128,128]{4,3,2,1,0:T(8,128)(2,1)}, bf16[1,2,2,128,128]{4,3,2,1,0:T(8,128)(2,1)S(1)}, u32[]{:S(2)}, u32[]{:S(2)}) %collective-permute-start) | collective-permute-done | bytes 131104 | tf_op jit(solution)/shard_map/ppermute | solution.py:15
  20.9 3.8 %collective-permute-start.2 = (bf16[3,1,2,128,128]{4,3,2,1,0:T(8,128)(2,1)S(1)}, bf16[3,1,2,128,128]{4,3,2,1,0:T(8,128)(2,1)S(1)}, u32[]{:S(2)}, u32[]{:S(2)}) collective-permute-start(bf16[3,1,2,128,128]{4,3,2,1,0:T(8,128)(2,1)S(1)} %get-tuple-element.30), channel_id=1, source_target_pairs={{0,16},{16,32},{32,48},{48,64},{64,80},{80,96},{96,112},{112,0},{1... | collective-permute-start | bytes 589832 | tf_op jit(solution)/shard_map/ppermute | solution.py:15
  24.7 1.3 collective-permute-start.3
  26.0 1.3 collective-permute-done.2
  27.3 2.8 %collective-permute-done.3 = bf16[3,1,2,128,128]{4,3,2,1,0:T(8,128)(2,1)S(1)} collective-permute-done((bf16[3,1,2,128,128]{4,3,2,1,0:T(8,128)(2,1)S(1)}, bf16[3,1,2,128,128]{4,3,2,1,0:T(8,128)(2,1)S(1)}, u32[]{:S(2)}, u32[]{:S(2)}) %collective-permute-start.3) | collective-permute-done | bytes 196640 | tf_op jit(solution)/shard_map/ppermute | solution.py:18
  30.3 3.3 %collective-permute-start.4 = (bf16[3,4,1,128,128]{4,3,2,1,0:T(8,128)(2,1)S(1)}, bf16[3,4,1,128,128]{4,3,2,1,0:T(8,128)(2,1)S(1)}, u32[]{:S(2)}, u32[]{:S(2)}) collective-permute-start(bf16[3,4,1,128,128]{4,3,2,1,0:T(8,128)(2,1)S(1)} %get-tuple-element.28), channel_id=1, source_target_pairs={{0,1},{1,2},{2,3},{3,4},{4,5},{5,6},{6,7},{7,8},{8,9},{9,10},{10,1... | collective-permute-start | bytes 1179656 | tf_op jit(solution)/shard_map/ppermute | solution.py:15
  33.5 9.5 %collective-permute-start.5 = (bf16[3,4,1,128,128]{4,3,2,1,0:T(8,128)(2,1)S(1)}, bf16[3,4,1,128,128]{4,3,2,1,0:T(8,128)(2,1)}, u32[]{:S(2)}, u32[]{:S(2)}) collective-permute-start(bf16[3,4,1,128,128]{4,3,2,1,0:T(8,128)(2,1)S(1)} %get-tuple-element.29), channel_id=1, source_target_pairs={{1,0},{2,1},{3,2},{4,3},{5,4},{6,5},{7,6},{8,7},{9,8},{10,9},{11,1... | collective-permute-start | bytes 1179656 | tf_op jit(solution)/shard_map/ppermute | solution.py:18
  43.2 7.2 %collective-permute-done.4 = bf16[3,4,1,128,128]{4,3,2,1,0:T(8,128)(2,1)S(1)} collective-permute-done((bf16[3,4,1,128,128]{4,3,2,1,0:T(8,128)(2,1)S(1)}, bf16[3,4,1,128,128]{4,3,2,1,0:T(8,128)(2,1)S(1)}, u32[]{:S(2)}, u32[]{:S(2)}) %collective-permute-start.4) | collective-permute-done | bytes 393248 | tf_op jit(solution)/shard_map/ppermute | solution.py:15
  51.4 1.3 pad_maximum_fusion
  52.7 1.6 %gather_fusion = bf16[28,128,128]{2,1,0:T(8,128)(2,1)} fusion(bf16[48,128,128]{2,1,0:T(8,128)(2,1)S(1)} %bitcast.94, s32[1024]{0:T(1024)S(1)} %pad_clamp_fusion.1), kind=kCustom, calls=%fused_computation | custom fusion | bytes 1835120 | tf_op jit(solution)/shard_map/gather | solution.py:88
  54.3 2.2 %convolution_bitcast_fusion.1 = f32[1,2,2,7,128,128]{4,5,3,2,1,0:T(8,128)S(1)} fusion(bf16[2,2,7,128,128]{4,3,2,1,0:T(8,128)(2,1)} %bitcast.96, bf16[1,2,2,7,128,128]{5,4,3,2,1,0:T(8,128)(2,1)S(1)} %copy-done, bf16[1,2,2,128,128]{4,3,2,1,0:T(8,128)(2,1)S(1)} %copy-done.1), kind=kOutput, calls=%fused_computation.11 | convolution fusion | flops 235339776 | bytes 3801088 | tf_op jit(solution)/shard_map/abcmn,abceml->abcenl/dot_general | solution.py:92
  57.6 2.7 %gather_fusion.1 = f32[14,128,128]{1,2,0:T(8,128)} fusion(f32[1,2,7,128,128]{3,4,2,1,0:T(8,128)} %slice_bitcast_fusion, s32[14]{0:T(128)S(1)} %reshape.407), kind=kCustom, calls=%fused_computation.1 | custom fusion | bytes 1835176 | tf_op jit(solution)/shard_map/gather | solution.py:126
  60.3 2.4 %copy.32 = f32[1,2,7,128,128]{4,3,1,2,0:T(8,128)} copy(f32[1,2,7,128,128]{3,4,2,1,0:T(8,128)} %bitcast.95) | data formatting | bytes 1835008 | tf_op jit(solution)/shard_map/gather | solution.py:126
  62.7 5.4 %collective-permute-start.6 = (f32[1,2,7,128,128]{4,3,1,2,0:T(8,128)}, f32[1,2,7,128,128]{4,3,1,2,0:T(8,128)}, u32[]{:S(2)}, u32[]{:S(2)}) collective-permute-start(f32[1,2,7,128,128]{4,3,1,2,0:T(8,128)} %copy.32), channel_id=1, source_target_pairs={{1,0},{2,1},{3,2},{4,3},{5,4},{6,5},{7,6},{8,7},{9,8},{10,9},{11,1... | collective-permute-start | bytes 2752520 | tf_op jit(solution)/shard_map/ppermute | solution.py:26
  68.2 1.1 collective-permute-start.9
  70.1 2.6 %collective-permute-done.10 = f32[3,1,1,128]{3,2,1,0:T(1,128)S(1)} collective-permute-done((f32[3,1,1,128]{3,2,1,0:T(1,128)S(1)}, f32[3,1,1,128]{3,2,1,0:T(1,128)S(1)}, u32[]{:S(2)}, u32[]{:S(2)}) %collective-permute-start.10) | collective-permute-done | bytes 1568 | tf_op jit(solution)/shard_map/ppermute | solution.py:18
  72.7 2.6 %collective-permute-start.12 = (f32[3,4,1,128]{3,2,1,0:T(1,128)S(1)}, f32[3,4,1,128]{3,2,1,0:T(1,128)S(1)}, u32[]{:S(2)}, u32[]{:S(2)}) collective-permute-start(f32[3,4,1,128]{3,2,1,0:T(1,128)S(1)} %pad_maximum_fusion.5), channel_id=1, source_target_pairs={{1,0},{2,1},{3,2},{4,3},{5,4},{6,5},{7,6},{8,7},{9,8},{10,9},{11,1... | collective-permute-start | bytes 18440 | tf_op jit(solution)/shard_map/ppermute | solution.py:18
  75.4 2.6 %collective-permute-start.11 = (f32[3,4,1,128]{3,2,1,0:T(1,128)S(1)}, f32[3,4,1,128]{3,2,1,0:T(1,128)S(1)}, u32[]{:S(2)}, u32[]{:S(2)}) collective-permute-start(f32[3,4,1,128]{3,2,1,0:T(1,128)S(1)} %pad_maximum_fusion.5), channel_id=1, source_target_pairs={{0,1},{1,2},{2,3},{3,4},{4,5},{5,6},{6,7},{7,8},{8,9},{9,10},{10,1... | collective-permute-start | bytes 18440 | tf_op jit(solution)/shard_map/ppermute | solution.py:15
  78.3 8.9 %collective-permute-done.12 = f32[3,4,1,128]{3,2,1,0:T(1,128)S(1)} collective-permute-done((f32[3,4,1,128]{3,2,1,0:T(1,128)S(1)}, f32[3,4,1,128]{3,2,1,0:T(1,128)S(1)}, u32[]{:S(2)}, u32[]{:S(2)}) %collective-permute-start.12) | collective-permute-done | bytes 6176 | tf_op jit(solution)/shard_map/ppermute | solution.py:18
  87.8 1.7 %copy.48 = f32[1,2,2,7,128,128]{5,4,3,2,1,0:T(8,128)} copy(f32[1,2,2,7,128,128]{4,5,3,2,1,0:T(8,128)S(1)} %convolution_bitcast_fusion.1) | data formatting | bytes 3670016 | tf_op jit(solution)/shard_map/reshape.66
  89.5 3.2 %reshape.462 = f32[2,14,16384]{2,1,0:T(8,128)} reshape(f32[1,2,2,7,128,128]{5,4,3,2,1,0:T(8,128)} %copy.48) | data formatting | bytes 3670016 | tf_op jit(solution)/shard_map/reshape.66
  92.7 2.7 %fusion.21 = f32[2,11,16384]{2,1,0:T(8,128)S(1)} fusion(f32[2,14,16384]{2,1,0:T(8,128)} %reshape.462, s32[2,14]{1,0:T(2,128)S(1)} %eq.138, pred[2,14]{1,0:T(4,128)(4,1)S(1)} %and.145), kind=kOutput, calls=%fused_computation.33 | convolution fusion | flops 60555880 | bytes 3276940 | tf_op jit(solution)/shard_map/abeq,abex->abqx/dot_general | solution.py:107
  95.4 2.7 %reshape.388 = f32[2,7,16384]{2,0,1:T(2,128)} reshape(f32[1,2,7,128,128]{4,3,1,2,0:T(8,128)} %collective-permute-done.6) | data formatting | bytes 1835008 | tf_op jit(solution)/shard_map/reshape.79
  98.1 4.5 %abs_reduce_fusion = (f32[2,16384]{1,0:T(2,128)S(1)}, f32[2,11,16384]{2,1,0:T(8,128)}) fusion(f32[2,11,16384]{2,1,0:T(8,128)S(1)} %fusion.21, f32[2]{0:T(128)S(1)} %compare_convert_fusion, s32[7]{0:T(128)S(1)} %compare_select_fusion.41, f32[2,7,16384]{2,0,1:T(2,128)} %reshape.388), kind=kOutput, calls=%fused_computation.9 | convolution fusion | flops 31686732 | bytes 3932196 | tf_op jit(solution)/shard_map/eq,abex->abqx/dot_general | solution.py:128
  102.7 1.9 %reshape.463 = f32[2,11,128,128]{3,2,1,0:T(8,128)S(1)} reshape(f32[2,11,16384]{2,1,0:T(8,128)} %get-tuple-element.41) | data formatting | bytes 2883584 | tf_op jit(solution)/shard_map/reshape.90
  104.6 1.4 fusion.8
  106.1 1.9 %collective-permute-start.14 = (f32[1,2,1,128]{3,1,2,0:T(2,128)S(1)}, f32[1,2,1,128]{3,1,2,0:T(2,128)S(1)}, u32[]{:S(2)}, u32[]{:S(2)}) collective-permute-start(f32[1,2,1,128]{3,1,2,0:T(2,128)S(1)} %fusion.65), channel_id=1, source_target_pairs={{128,0},{256,128},{384,256},{0,384},{129,1},{257,129},{385,257},{1... | collective-permute-start | bytes 3080 | tf_op jit(solution)/shard_map/ppermute | solution.py:18
  108.0 3.4 %collective-permute-start.13 = (f32[1,2,1,128]{3,1,2,0:T(2,128)S(1)}, f32[1,2,1,128]{3,1,2,0:T(2,128)S(1)}, u32[]{:S(2)}, u32[]{:S(2)}) collective-permute-start(f32[1,2,1,128]{3,1,2,0:T(2,128)S(1)} %fusion.65), channel_id=1, source_target_pairs={{0,128},{128,256},{256,384},{384,0},{1,129},{129,257},{257,385},{3... | collective-permute-start | bytes 3080 | tf_op jit(solution)/shard_map/ppermute | solution.py:15
  111.4 2.1 %collective-permute-done.13 = f32[1,2,1,128]{3,1,2,0:T(2,128)S(1)} collective-permute-done((f32[1,2,1,128]{3,1,2,0:T(2,128)S(1)}, f32[1,2,1,128]{3,1,2,0:T(2,128)S(1)}, u32[]{:S(2)}, u32[]{:S(2)}) %collective-permute-start.13) | collective-permute-done | bytes 1056 | tf_op jit(solution)/shard_map/ppermute | solution.py:15
  113.5 3.8 %collective-permute-start.15 = (f32[3,1,1,128]{3,1,2,0:T(1,128)S(1)}, f32[3,1,1,128]{3,1,2,0:T(1,128)S(1)}, u32[]{:S(2)}, u32[]{:S(2)}) collective-permute-start(f32[3,1,1,128]{3,1,2,0:T(1,128)S(1)} %get-tuple-element.34), channel_id=1, source_target_pairs={{0,16},{16,32},{32,48},{48,64},{64,80},{80,96},{96,112},{112,0},{1... | collective-permute-start | bytes 4616 | tf_op jit(solution)/shard_map/ppermute | solution.py:15
  118.0 2.4 %collective-permute-done.16 = f32[3,1,1,128]{3,1,2,0:T(1,128)S(1)} collective-permute-done((f32[3,1,1,128]{3,1,2,0:T(1,128)S(1)}, f32[3,1,1,128]{3,1,2,0:T(1,128)S(1)}, u32[]{:S(2)}, u32[]{:S(2)}) %collective-permute-start.16) | collective-permute-done | bytes 1568 | tf_op jit(solution)/shard_map/ppermute | solution.py:18
  120.4 5.3 %collective-permute-start.18 = (f32[3,4,1,128]{3,1,2,0:T(4,128)S(1)}, f32[3,4,1,128]{3,1,2,0:T(4,128)S(1)}, u32[]{:S(2)}, u32[]{:S(2)}) collective-permute-start(f32[3,4,1,128]{3,1,2,0:T(4,128)S(1)} %pad_maximum_fusion.6), channel_id=1, source_target_pairs={{1,0},{2,1},{3,2},{4,3},{5,4},{6,5},{7,6},{8,7},{9,8},{10,9},{11,1... | collective-permute-start | bytes 18440 | tf_op jit(solution)/shard_map/ppermute | solution.py:18
  125.7 1.9 %collective-permute-start.17 = (f32[3,4,1,128]{3,1,2,0:T(4,128)S(1)}, f32[3,4,1,128]{3,1,2,0:T(4,128)S(1)}, u32[]{:S(2)}, u32[]{:S(2)}) collective-permute-start(f32[3,4,1,128]{3,1,2,0:T(4,128)S(1)} %pad_maximum_fusion.6), channel_id=1, source_target_pairs={{0,1},{1,2},{2,3},{3,4},{4,5},{5,6},{6,7},{7,8},{8,9},{9,10},{10,1... | collective-permute-start | bytes 18440 | tf_op jit(solution)/shard_map/ppermute | solution.py:15
  127.7 3.6 %collective-permute-done.17 = f32[3,4,1,128]{3,1,2,0:T(4,128)S(1)} collective-permute-done((f32[3,4,1,128]{3,1,2,0:T(4,128)S(1)}, f32[3,4,1,128]{3,1,2,0:T(4,128)S(1)}, u32[]{:S(2)}, u32[]{:S(2)}) %collective-permute-start.17) | collective-permute-done | bytes 6176 | tf_op jit(solution)/shard_map/ppermute | solution.py:15
  131.9 1.4 fusion.6
  133.4 1.9 %collective-permute-start.20 = (f32[1,2,1,128]{3,1,2,0:T(2,128)S(1)}, f32[1,2,1,128]{3,1,2,0:T(2,128)S(1)}, u32[]{:S(2)}, u32[]{:S(2)}) collective-permute-start(f32[1,2,1,128]{3,1,2,0:T(2,128)S(1)} %fusion.66), channel_id=1, source_target_pairs={{128,0},{256,128},{384,256},{0,384},{129,1},{257,129},{385,257},{1... | collective-permute-start | bytes 3080 | tf_op jit(solution)/shard_map/ppermute | solution.py:18
  135.3 3.4 %collective-permute-start.19 = (f32[1,2,1,128]{3,1,2,0:T(2,128)S(1)}, f32[1,2,1,128]{3,1,2,0:T(2,128)S(1)}, u32[]{:S(2)}, u32[]{:S(2)}) collective-permute-start(f32[1,2,1,128]{3,1,2,0:T(2,128)S(1)} %fusion.66), channel_id=1, source_target_pairs={{0,128},{128,256},{256,384},{384,0},{1,129},{129,257},{257,385},{3... | collective-permute-start | bytes 3080 | tf_op jit(solution)/shard_map/ppermute | solution.py:15
  138.7 2.1 %collective-permute-done.19 = f32[1,2,1,128]{3,1,2,0:T(2,128)S(1)} collective-permute-done((f32[1,2,1,128]{3,1,2,0:T(2,128)S(1)}, f32[1,2,1,128]{3,1,2,0:T(2,128)S(1)}, u32[]{:S(2)}, u32[]{:S(2)}) %collective-permute-start.19) | collective-permute-done | bytes 1056 | tf_op jit(solution)/shard_map/ppermute | solution.py:15
  140.8 2.6 %collective-permute-start.21 = (f32[3,1,1,128]{3,1,2,0:T(1,128)S(1)}, f32[3,1,1,128]{3,1,2,0:T(1,128)S(1)}, u32[]{:S(2)}, u32[]{:S(2)}) collective-permute-start(f32[3,1,1,128]{3,1,2,0:T(1,128)S(1)} %get-tuple-element.32), channel_id=1, source_target_pairs={{0,16},{16,32},{32,48},{48,64},{64,80},{80,96},{96,112},{112,0},{1... | collective-permute-start | bytes 4616 | tf_op jit(solution)/shard_map/ppermute | solution.py:15
  144.5 1.9 %collective-permute-done.22 = f32[3,1,1,128]{3,1,2,0:T(1,128)S(1)} collective-permute-done((f32[3,1,1,128]{3,1,2,0:T(1,128)S(1)}, f32[3,1,1,128]{3,1,2,0:T(1,128)S(1)}, u32[]{:S(2)}, u32[]{:S(2)}) %collective-permute-start.22) | collective-permute-done | bytes 1568 | tf_op jit(solution)/shard_map/ppermute | solution.py:18
  146.4 1.9 %collective-permute-start.24 = (f32[3,4,1,128]{3,1,2,0:T(4,128)S(1)}, f32[3,4,1,128]{3,1,2,0:T(4,128)S(1)}, u32[]{:S(2)}, u32[]{:S(2)}) collective-permute-start(f32[3,4,1,128]{3,1,2,0:T(4,128)S(1)} %pad_maximum_fusion.7), channel_id=1, source_target_pairs={{1,0},{2,1},{3,2},{4,3},{5,4},{6,5},{7,6},{8,7},{9,8},{10,9},{11,1... | collective-permute-start | bytes 18440 | tf_op jit(solution)/shard_map/ppermute | solution.py:18
  148.3 3.4 %collective-permute-start.23 = (f32[3,4,1,128]{3,1,2,0:T(4,128)S(1)}, f32[3,4,1,128]{3,1,2,0:T(4,128)S(1)}, u32[]{:S(2)}, u32[]{:S(2)}) collective-permute-start(f32[3,4,1,128]{3,1,2,0:T(4,128)S(1)} %pad_maximum_fusion.7), channel_id=1, source_target_pairs={{0,1},{1,2},{2,3},{3,4},{4,5},{5,6},{6,7},{7,8},{8,9},{9,10},{10,1... | collective-permute-start | bytes 18440 | tf_op jit(solution)/shard_map/ppermute | solution.py:15
  151.7 2.2 %collective-permute-done.23 = f32[3,4,1,128]{3,1,2,0:T(4,128)S(1)} collective-permute-done((f32[3,4,1,128]{3,1,2,0:T(4,128)S(1)}, f32[3,4,1,128]{3,1,2,0:T(4,128)S(1)}, u32[]{:S(2)}, u32[]{:S(2)}) %collective-permute-start.23) | collective-permute-done | bytes 6176 | tf_op jit(solution)/shard_map/ppermute | solution.py:15
  154.6 2.0 %fusion.13 = f32[1,2,1,128]{3,2,1,0:T(1,128)} fusion(f32[1,2,1,128]{3,2,1,0:T(1,128)S(1)} %copy-done.4, f32[2,11,128,128]{3,2,1,0:T(8,128)S(1)} %reshape.463, f32[2,11,128,1]{2,1,0,3:T(8,128)S(1)} %reshape.460), kind=kOutput, calls=%fused_computation.21 | convolution fusion | flops 4325632 | bytes 1455104 | tf_op jit(solution)/shard_map/abcsij,abcsj->abci/dot_general | solution.py:58
  (90 shorter events, 11.2 us)
Async XLA Ops:
  0.6 53.7 %copy-start = (bf16[1,2,2,7,128,128]{5,4,3,2,1,0:T(8,128)(2,1)S(1)}, bf16[1,2,2,7,128,128]{5,4,3,2,1,0:T(8,128)(2,1)}, u32[]{:S(2)}) copy-start(bf16[1,2,2,7,128,128]{5,4,3,2,1,0:T(8,128)(2,1)} %param.9) | copy-start | bytes 2752516
  0.6 42.6 %collective-permute-start.8 = (f32[1,2,1,128]{3,2,1,0:T(1,128)}, f32[1,2,1,128]{3,2,1,0:T(1,128)S(1)}, u32[]{:S(2)}, u32[]{:S(2)}) collective-permute-start(f32[1,2,1,128]{3,2,1,0:T(1,128)} %param.15), channel_id=1, source_target_pairs={{128,0},{256,128},{384,256},{0,384},{129,1},{257,129},{385,257},{1... | collective-permute-start | bytes 3080 | tf_op jit(solution)/shard_map/ppermute | solution.py:18
  6.3 36.9 %collective-permute-start.7 = (f32[1,2,1,128]{3,2,1,0:T(1,128)}, f32[1,2,1,128]{3,2,1,0:T(1,128)S(1)}, u32[]{:S(2)}, u32[]{:S(2)}) collective-permute-start(f32[1,2,1,128]{3,2,1,0:T(1,128)} %param.15), channel_id=1, source_target_pairs={{0,128},{128,256},{256,384},{384,0},{1,129},{129,257},{257,385},{3... | collective-permute-start | bytes 3080 | tf_op jit(solution)/shard_map/ppermute | solution.py:15
  8.2 12.7 %collective-permute-start.1 = (bf16[1,2,2,128,128]{4,3,2,1,0:T(8,128)(2,1)}, bf16[1,2,2,128,128]{4,3,2,1,0:T(8,128)(2,1)S(1)}, u32[]{:S(2)}, u32[]{:S(2)}) collective-permute-start(bf16[1,2,2,128,128]{4,3,2,1,0:T(8,128)(2,1)} %param.11), channel_id=1, source_target_pairs={{128,0},{256,128},{384,256},{0,384},{129,1},{257,129},{385,257},{1... | collective-permute-start | bytes 393224 | tf_op jit(solution)/shard_map/ppermute | solution.py:18
  12.8 7.1 %collective-permute-start = (bf16[1,2,2,128,128]{4,3,2,1,0:T(8,128)(2,1)}, bf16[1,2,2,128,128]{4,3,2,1,0:T(8,128)(2,1)S(1)}, u32[]{:S(2)}, u32[]{:S(2)}) collective-permute-start(bf16[1,2,2,128,128]{4,3,2,1,0:T(8,128)(2,1)} %param.11), channel_id=1, source_target_pairs={{0,128},{128,256},{256,384},{384,0},{1,129},{129,257},{257,385},{3... | collective-permute-start | bytes 393224 | tf_op jit(solution)/shard_map/ppermute | solution.py:15
  20.9 6.4 %collective-permute-start.2 = (bf16[3,1,2,128,128]{4,3,2,1,0:T(8,128)(2,1)S(1)}, bf16[3,1,2,128,128]{4,3,2,1,0:T(8,128)(2,1)S(1)}, u32[]{:S(2)}, u32[]{:S(2)}) collective-permute-start(bf16[3,1,2,128,128]{4,3,2,1,0:T(8,128)(2,1)S(1)} %get-tuple-element.30), channel_id=1, source_target_pairs={{0,16},{16,32},{32,48},{48,64},{64,80},{80,96},{96,112},{112,0},{1... | collective-permute-start | bytes 589832 | tf_op jit(solution)/shard_map/ppermute | solution.py:15
  24.7 5.4 %collective-permute-start.3 = (bf16[3,1,2,128,128]{4,3,2,1,0:T(8,128)(2,1)S(1)}, bf16[3,1,2,128,128]{4,3,2,1,0:T(8,128)(2,1)S(1)}, u32[]{:S(2)}, u32[]{:S(2)}) collective-permute-start(bf16[3,1,2,128,128]{4,3,2,1,0:T(8,128)(2,1)S(1)} %get-tuple-element.31), channel_id=1, source_target_pairs={{16,0},{32,16},{48,32},{64,48},{80,64},{96,80},{112,96},{0,112},{1... | collective-permute-start | bytes 589832 | tf_op jit(solution)/shard_map/ppermute | solution.py:18
  26.0 17.2 %copy-start.5 = (f32[1,2,1,128]{3,2,1,0:T(1,128)S(1)}, f32[1,2,1,128]{3,2,1,0:T(1,128)}, u32[]{:S(2)}) copy-start(f32[1,2,1,128]{3,2,1,0:T(1,128)} %param.15) | copy-start | bytes 3076
  30.3 20.2 %collective-permute-start.4 = (bf16[3,4,1,128,128]{4,3,2,1,0:T(8,128)(2,1)S(1)}, bf16[3,4,1,128,128]{4,3,2,1,0:T(8,128)(2,1)S(1)}, u32[]{:S(2)}, u32[]{:S(2)}) collective-permute-start(bf16[3,4,1,128,128]{4,3,2,1,0:T(8,128)(2,1)S(1)} %get-tuple-element.28), channel_id=1, source_target_pairs={{0,1},{1,2},{2,3},{3,4},{4,5},{5,6},{6,7},{7,8},{8,9},{9,10},{10,1... | collective-permute-start | bytes 1179656 | tf_op jit(solution)/shard_map/ppermute | solution.py:15
  33.5 17.9 %collective-permute-start.5 = (bf16[3,4,1,128,128]{4,3,2,1,0:T(8,128)(2,1)S(1)}, bf16[3,4,1,128,128]{4,3,2,1,0:T(8,128)(2,1)}, u32[]{:S(2)}, u32[]{:S(2)}) collective-permute-start(bf16[3,4,1,128,128]{4,3,2,1,0:T(8,128)(2,1)S(1)} %get-tuple-element.29), channel_id=1, source_target_pairs={{1,0},{2,1},{3,2},{4,3},{5,4},{6,5},{7,6},{8,7},{9,8},{10,9},{11,1... | collective-permute-start | bytes 1179656 | tf_op jit(solution)/shard_map/ppermute | solution.py:18
  50.4 0.7 copy-start.2
  52.7 1.6 %copy-start.1 = (bf16[1,2,2,128,128]{4,3,2,1,0:T(8,128)(2,1)S(1)}, bf16[1,2,2,128,128]{4,3,2,1,0:T(8,128)(2,1)}, u32[]{:S(2)}) copy-start(bf16[1,2,2,128,128]{4,3,2,1,0:T(8,128)(2,1)} %param.11) | copy-start | bytes 393220
  62.7 32.7 %collective-permute-start.6 = (f32[1,2,7,128,128]{4,3,1,2,0:T(8,128)}, f32[1,2,7,128,128]{4,3,1,2,0:T(8,128)}, u32[]{:S(2)}, u32[]{:S(2)}) collective-permute-start(f32[1,2,7,128,128]{4,3,1,2,0:T(8,128)} %copy.32), channel_id=1, source_target_pairs={{1,0},{2,1},{3,2},{4,3},{5,4},{6,5},{7,6},{8,7},{9,8},{10,9},{11,1... | collective-permute-start | bytes 2752520 | tf_op jit(solution)/shard_map/ppermute | solution.py:26
  68.2 1.9 %collective-permute-start.9 = (f32[3,1,1,128]{3,2,1,0:T(1,128)S(1)}, f32[3,1,1,128]{3,2,1,0:T(1,128)S(1)}, u32[]{:S(2)}, u32[]{:S(2)}) collective-permute-start(f32[3,1,1,128]{3,2,1,0:T(1,128)S(1)} %get-tuple-element.36), channel_id=1, source_target_pairs={{0,16},{16,32},{32,48},{48,64},{64,80},{80,96},{96,112},{112,0},{1... | collective-permute-start | bytes 4616 | tf_op jit(solution)/shard_map/ppermute | solution.py:15
  69.3 3.4 %collective-permute-start.10 = (f32[3,1,1,128]{3,2,1,0:T(1,128)S(1)}, f32[3,1,1,128]{3,2,1,0:T(1,128)S(1)}, u32[]{:S(2)}, u32[]{:S(2)}) collective-permute-start(f32[3,1,1,128]{3,2,1,0:T(1,128)S(1)} %get-tuple-element.37), channel_id=1, source_target_pairs={{16,0},{32,16},{48,32},{64,48},{80,64},{96,80},{112,96},{0,112},{1... | collective-permute-start | bytes 4616 | tf_op jit(solution)/shard_map/ppermute | solution.py:18
  72.7 14.5 %collective-permute-start.12 = (f32[3,4,1,128]{3,2,1,0:T(1,128)S(1)}, f32[3,4,1,128]{3,2,1,0:T(1,128)S(1)}, u32[]{:S(2)}, u32[]{:S(2)}) collective-permute-start(f32[3,4,1,128]{3,2,1,0:T(1,128)S(1)} %pad_maximum_fusion.5), channel_id=1, source_target_pairs={{1,0},{2,1},{3,2},{4,3},{5,4},{6,5},{7,6},{8,7},{9,8},{10,9},{11,1... | collective-permute-start | bytes 18440 | tf_op jit(solution)/shard_map/ppermute | solution.py:18
  75.4 11.9 %collective-permute-start.11 = (f32[3,4,1,128]{3,2,1,0:T(1,128)S(1)}, f32[3,4,1,128]{3,2,1,0:T(1,128)S(1)}, u32[]{:S(2)}, u32[]{:S(2)}) collective-permute-start(f32[3,4,1,128]{3,2,1,0:T(1,128)S(1)} %pad_maximum_fusion.5), channel_id=1, source_target_pairs={{0,1},{1,2},{2,3},{3,4},{4,5},{5,6},{6,7},{7,8},{8,9},{9,10},{10,1... | collective-permute-start | bytes 18440 | tf_op jit(solution)/shard_map/ppermute | solution.py:15
  102.7 3.4 %copy-start.4 = (f32[1,2,1,128]{3,2,1,0:T(1,128)S(1)}, f32[1,2,1,128]{3,2,1,0:T(1,128)}, u32[]{:S(2)}) copy-start(f32[1,2,1,128]{3,2,1,0:T(1,128)} %param.14) | copy-start | bytes 3076
  106.1 5.3 %collective-permute-start.14 = (f32[1,2,1,128]{3,1,2,0:T(2,128)S(1)}, f32[1,2,1,128]{3,1,2,0:T(2,128)S(1)}, u32[]{:S(2)}, u32[]{:S(2)}) collective-permute-start(f32[1,2,1,128]{3,1,2,0:T(2,128)S(1)} %fusion.65), channel_id=1, source_target_pairs={{128,0},{256,128},{384,256},{0,384},{129,1},{257,129},{385,257},{1... | collective-permute-start | bytes 3080 | tf_op jit(solution)/shard_map/ppermute | solution.py:18
  108.0 5.5 %collective-permute-start.13 = (f32[1,2,1,128]{3,1,2,0:T(2,128)S(1)}, f32[1,2,1,128]{3,1,2,0:T(2,128)S(1)}, u32[]{:S(2)}, u32[]{:S(2)}) collective-permute-start(f32[1,2,1,128]{3,1,2,0:T(2,128)S(1)} %fusion.65), channel_id=1, source_target_pairs={{0,128},{128,256},{256,384},{384,0},{1,129},{129,257},{257,385},{3... | collective-permute-start | bytes 3080 | tf_op jit(solution)/shard_map/ppermute | solution.py:15
  113.5 4.5 %collective-permute-start.15 = (f32[3,1,1,128]{3,1,2,0:T(1,128)S(1)}, f32[3,1,1,128]{3,1,2,0:T(1,128)S(1)}, u32[]{:S(2)}, u32[]{:S(2)}) collective-permute-start(f32[3,1,1,128]{3,1,2,0:T(1,128)S(1)} %get-tuple-element.34), channel_id=1, source_target_pairs={{0,16},{16,32},{32,48},{48,64},{64,80},{80,96},{96,112},{112,0},{1... | collective-permute-start | bytes 4616 | tf_op jit(solution)/shard_map/ppermute | solution.py:15
  117.3 3.1 %collective-permute-start.16 = (f32[3,1,1,128]{3,1,2,0:T(1,128)S(1)}, f32[3,1,1,128]{3,1,2,0:T(1,128)S(1)}, u32[]{:S(2)}, u32[]{:S(2)}) collective-permute-start(f32[3,1,1,128]{3,1,2,0:T(1,128)S(1)} %get-tuple-element.35), channel_id=1, source_target_pairs={{16,0},{32,16},{48,32},{64,48},{80,64},{96,80},{112,96},{0,112},{1... | collective-permute-start | bytes 4616 | tf_op jit(solution)/shard_map/ppermute | solution.py:18
  120.4 7.3 %collective-permute-start.18 = (f32[3,4,1,128]{3,1,2,0:T(4,128)S(1)}, f32[3,4,1,128]{3,1,2,0:T(4,128)S(1)}, u32[]{:S(2)}, u32[]{:S(2)}) collective-permute-start(f32[3,4,1,128]{3,1,2,0:T(4,128)S(1)} %pad_maximum_fusion.6), channel_id=1, source_target_pairs={{1,0},{2,1},{3,2},{4,3},{5,4},{6,5},{7,6},{8,7},{9,8},{10,9},{11,1... | collective-permute-start | bytes 18440 | tf_op jit(solution)/shard_map/ppermute | solution.py:18
  125.7 5.6 %collective-permute-start.17 = (f32[3,4,1,128]{3,1,2,0:T(4,128)S(1)}, f32[3,4,1,128]{3,1,2,0:T(4,128)S(1)}, u32[]{:S(2)}, u32[]{:S(2)}) collective-permute-start(f32[3,4,1,128]{3,1,2,0:T(4,128)S(1)} %pad_maximum_fusion.6), channel_id=1, source_target_pairs={{0,1},{1,2},{2,3},{3,4},{4,5},{5,6},{6,7},{7,8},{8,9},{9,10},{10,1... | collective-permute-start | bytes 18440 | tf_op jit(solution)/shard_map/ppermute | solution.py:15
  133.4 23.2 %copy-start.3 = (f32[1,2,1,128]{3,1,2,0:T(2,128)}, f32[1,2,1,128]{3,1,2,0:T(2,128)S(1)}, u32[]{:S(2)}) copy-start(f32[1,2,1,128]{3,1,2,0:T(2,128)S(1)} %fusion.66) | copy-start | bytes 3076
  133.4 5.3 %collective-permute-start.20 = (f32[1,2,1,128]{3,1,2,0:T(2,128)S(1)}, f32[1,2,1,128]{3,1,2,0:T(2,128)S(1)}, u32[]{:S(2)}, u32[]{:S(2)}) collective-permute-start(f32[1,2,1,128]{3,1,2,0:T(2,128)S(1)} %fusion.66), channel_id=1, source_target_pairs={{128,0},{256,128},{384,256},{0,384},{129,1},{257,129},{385,257},{1... | collective-permute-start | bytes 3080 | tf_op jit(solution)/shard_map/ppermute | solution.py:18
  135.3 5.5 %collective-permute-start.19 = (f32[1,2,1,128]{3,1,2,0:T(2,128)S(1)}, f32[1,2,1,128]{3,1,2,0:T(2,128)S(1)}, u32[]{:S(2)}, u32[]{:S(2)}) collective-permute-start(f32[1,2,1,128]{3,1,2,0:T(2,128)S(1)} %fusion.66), channel_id=1, source_target_pairs={{0,128},{128,256},{256,384},{384,0},{1,129},{129,257},{257,385},{3... | collective-permute-start | bytes 3080 | tf_op jit(solution)/shard_map/ppermute | solution.py:15
  140.8 3.7 %collective-permute-start.21 = (f32[3,1,1,128]{3,1,2,0:T(1,128)S(1)}, f32[3,1,1,128]{3,1,2,0:T(1,128)S(1)}, u32[]{:S(2)}, u32[]{:S(2)}) collective-permute-start(f32[3,1,1,128]{3,1,2,0:T(1,128)S(1)} %get-tuple-element.32), channel_id=1, source_target_pairs={{0,16},{16,32},{32,48},{48,64},{64,80},{80,96},{96,112},{112,0},{1... | collective-permute-start | bytes 4616 | tf_op jit(solution)/shard_map/ppermute | solution.py:15
  143.4 3.0 %collective-permute-start.22 = (f32[3,1,1,128]{3,1,2,0:T(1,128)S(1)}, f32[3,1,1,128]{3,1,2,0:T(1,128)S(1)}, u32[]{:S(2)}, u32[]{:S(2)}) collective-permute-start(f32[3,1,1,128]{3,1,2,0:T(1,128)S(1)} %get-tuple-element.33), channel_id=1, source_target_pairs={{16,0},{32,16},{48,32},{64,48},{80,64},{96,80},{112,96},{0,112},{1... | collective-permute-start | bytes 4616 | tf_op jit(solution)/shard_map/ppermute | solution.py:18
  146.4 5.3 %collective-permute-start.24 = (f32[3,4,1,128]{3,1,2,0:T(4,128)S(1)}, f32[3,4,1,128]{3,1,2,0:T(4,128)S(1)}, u32[]{:S(2)}, u32[]{:S(2)}) collective-permute-start(f32[3,4,1,128]{3,1,2,0:T(4,128)S(1)} %pad_maximum_fusion.7), channel_id=1, source_target_pairs={{1,0},{2,1},{3,2},{4,3},{5,4},{6,5},{7,6},{8,7},{9,8},{10,9},{11,1... | collective-permute-start | bytes 18440 | tf_op jit(solution)/shard_map/ppermute | solution.py:18
  148.3 5.6 %collective-permute-start.23 = (f32[3,4,1,128]{3,1,2,0:T(4,128)S(1)}, f32[3,4,1,128]{3,1,2,0:T(4,128)S(1)}, u32[]{:S(2)}, u32[]{:S(2)}) collective-permute-start(f32[3,4,1,128]{3,1,2,0:T(4,128)S(1)} %pad_maximum_fusion.7), channel_id=1, source_target_pairs={{0,1},{1,2},{2,3},{3,4},{4,5},{5,6},{6,7},{7,8},{8,9},{9,10},{10,1... | collective-permute-start | bytes 18440 | tf_op jit(solution)/shard_map/ppermute | solution.py:15
where the time goes:
time: 158 us; the launch traced here: 157 us
  starting transfers between devices  73.7 us (47%)
  waiting for transfers between devices  41.6 us (26%)
  local copies, waits for them, and re-layouts  21.5 us (14%)
  matrix products  14.1 us (9%)
  other arithmetic  4.45 us (3%)
    ppermute x12, starting transfers between devices, extended(): lax.ppermute(lax.slice_in_dim(block, 0, width, axis=dim), axis, backward)  35.3 us
    ppermute x12, starting transfers between devices, extended(): lax.ppermute(lax.slice_in_dim(block, block.shape[dim] - width, None, axis...  33 us
    ppermute x12, waiting for transfers between devices, extended(): lax.ppermute(lax.slice_in_dim(block, block.shape[dim] - width, None, axis...  22.8 us
    ppermute x12, waiting for transfers between devices, extended(): lax.ppermute(lax.slice_in_dim(block, 0, width, axis=dim), axis, backward)  18.8 us
    another operation x8, local copies, waits for them, and re-layouts  9.52 us
    ppermute x1, starting transfers between devices, shifted(): return lax.ppermute(block, axis, route)  5.42 us
    gather x2, local copies, waits for them, and re-layouts, body(): arrived = shifted(pieces[:, :, 0][row_x, row_y, order], 'gz', -1)  5.15 us
    dot_general x3, matrix products, apply_coarse(): jnp.einsum('abcsij,abcsj->abci', operator, picked, precision=lax.Precisio...  4.79 us
  transfers between devices with their start and end apart: 25, of which 16 were waited for; matrix products, arithmetic and copies ran while one was open for 8% of the time, Pallas kernels for 0%

commit v1 on v0

v1 whole, which is shorter than its diff:
```python
import jax
import jax.numpy as jnp
from jax import lax
from jax.experimental import pallas as pl
from jax.experimental.pallas import tpu as pltpu
from jax.sharding import PartitionSpec as P

EPSILON = 1e-05
MESH = pl.DeviceIdType.MESH
F32 = jnp.float32
BF16 = jnp.bfloat16
N = 128
SELF, ZM, ZP, XM, XP, YM, YP = range(7)
OWN, ZED = 0, 1
LATERAL = ((-1, 0), (1, 0), (0, -1), (0, 1))
RELATIONS = (
    [(dx, dy, 0) for dx, dy in LATERAL]
    + [(0, 0, -1), (0, 0, 1)]
    + [(dx, dy, dz) for dx, dy in LATERAL for dz in (-1, 1)]
)


def opposite(r):
    return RELATIONS.index(tuple(-d for d in RELATIONS[r]))


START_TO = [0, 1, 2, 3, 4, 5, 7, 9, 11, 13]
START_FROM = [opposite(r) for r in START_TO]


def kernel(
    a_hbm, cols_ref, p_hbm, agg_ref, rhs_ref, start_ref,
    sol_ref, res_ref,
    a_v, p_v, px, py, pz, stage, partner, pieces, acc_y, acc_a,
    w_ref, m0, r0, f1, s1, r1, inv_ref, f2, s2, r2, s3, r3,
    a_sem, p_sem, bulk_send, bulk_recv, small_send, small_recv,
):
    gx, gy, gz = lax.axis_index("gx"), lax.axis_index("gy"), lax.axis_index("gz")
    nx, ny, nz = lax.axis_size("gx"), lax.axis_size("gy"), lax.axis_size("gz")
    total_y, total_z = 2 * ny, 2 * nz

    def device(r):
        dx, dy, dz = RELATIONS[r]
        return (
            lax.rem(gx + dx + nx, nx) if dx else gx,
            lax.rem(gy + dy + ny, ny) if dy else gy,
            lax.rem(gz + dz + nz, nz) if dz else gz,
        )

    devices = [device(r) for r in range(14)]
    barrier = pltpu.get_barrier_semaphore()
    for r in range(14):
        pl.semaphore_signal(barrier, inc=1, device_id=devices[r], device_id_type=MESH)

    p_copy = pltpu.make_async_copy(p_hbm.at[0], p_v, p_sem)
    p_copy.start()
    a_copy = pltpu.make_async_copy(a_hbm.at[0], a_v, a_sem)
    a_copy.start()

    phase = [
        (agg_ref[0, c, 0] != (gx * total_y + 2 * gy + c) * nz + gz).astype(jnp.int32)
        for c in (0, 1)
    ]

    def place(c, j, d):
        dx = {XM: -1, XP: 1}.get(d, 0)
        dy = {YM: -1, YP: 1}.get(d, 0)
        dz = {ZM: -1, ZP: 1}.get(d, 0)
        x = lax.rem(gx + dx + nx, nx)
        y = lax.rem(2 * gy + c + dy + total_y, total_y)
        z = lax.rem(2 * gz + j + dz + total_z, total_z)
        want = (x * total_y + y) * total_z + z
        found = jnp.int32(0)
        for e in range(1, 7):
            found = jnp.where(cols_ref[0, c, j, e] == want, e, found)
        return found

    row8 = lax.broadcasted_iota(jnp.int32, (8, N), 0)
    even8 = lax.rem(row8, 2) == 0
    even4 = even8[0:4]
    ph8 = jnp.where(lax.rem(row8, 4) < 2, phase[0], phase[1]).astype(F32)
    ph4 = ph8[0:4]
    straddle8 = ph8 > 0.5
    straddle4 = ph4 > 0.5
    start = start_ref[0, :, 0, :]
    for c in (0, 1):
        m0[0, 2 * c : 2 * c + 1, :] = start[c : c + 1]
        m0[0, 2 * c + 1 : 2 * c + 2, :] = start[c : c + 1]
    m0[0, 4:8, :] = jnp.zeros((4, N), F32)
    m0[1] = ph8

    pl.semaphore_wait(barrier, 14)

    small = [
        pltpu.make_async_remote_copy(
            m0, r0.at[START_FROM.index(opposite(r))], small_send.at[0], small_recv.at[0],
            device_id=devices[r], device_id_type=MESH,
        )
        for r in START_TO
    ]
    for copy in small:
        copy.start()

    def bulk(k, source, target, r):
        return pltpu.make_async_remote_copy(
            source, target, bulk_send.at[k], bulk_recv.at[k],
            device_id=devices[r], device_id_type=MESH,
        )

    sends = [
        bulk(0, p_hbm.at[0, :, 1], pz.at[0], 5),
        bulk(1, p_hbm.at[0, :, 0], pz.at[1], 4),
        bulk(2, p_hbm.at[0], px.at[0], 1),
        bulk(3, p_hbm.at[0], px.at[1], 0),
        bulk(4, p_hbm.at[0, 1], py.at[0], 3),
        bulk(5, p_hbm.at[0, 0], py.at[1], 2),
        bulk(6, stage.at[0], partner.at[0], 4),
        bulk(7, stage.at[1], partner.at[1], 5),
    ]
    for copy in sends[:6]:
        copy.start()

    where = [[[place(c, j, d) for d in range(7)] for j in (0, 1)] for c in (0, 1)]

    a_copy.wait()
    stage[0, 0] = a_v[0, 0, where[0][0][SELF]]
    stage[0, 1] = a_v[0, 0, where[0][0][ZM]]
    stage[1, 0] = a_v[1, 1, where[1][1][SELF]]
    stage[1, 1] = a_v[1, 1, where[1][1][ZP]]
    sends[6].start()
    sends[7].start()

    pltpu.make_async_copy(r0, r0, small_recv.at[0]).wait()
    below, above = r0[START_FROM.index(4), 0, 0:4], r0[START_FROM.index(5), 0, 0:4]
    mine = m0[0, 0:4]
    w_ref[OWN, 0:4] = jnp.where(straddle4 & even4, below, mine)
    w_ref[ZED, 0:4] = jnp.where(even4, below, jnp.where(straddle4, mine, above))
    for l in range(4):
        side = START_FROM.index(l)
        far = START_FROM.index(6 + 2 * l)
        moved = (r0[side, 1, 0:4] > 0.5) & even4
        w_ref[2 + l, 0:4] = jnp.where(moved, r0[far, 0, 0:4], r0[side, 0, 0:4])

    def vector(c, j, d):
        t = 2 * c + j
        if d == SELF:
            block, row = OWN, t
        elif d in (ZM, ZP):
            inner = (d == ZP) == (j == 0)
            block, row = (OWN, 2 * c + 1 - j) if inner else (ZED, t)
        elif d in (XM, XP):
            block, row = 2 + (d - XM), t
        else:
            inner = (d == YP) == (c == 0)
            block, row = (OWN, 2 * (1 - c) + j) if inner else (4 + (d - YM), 2 * (1 - c) + j)
        return w_ref[block, row : row + 1, :]

    def near(c, j, d):
        if d == SELF:
            return p_v[c, j]
        if d in (ZM, ZP):
            inner = (d == ZP) == (j == 0)
            return p_v[c, 1 - j] if inner else pz[0 if d == ZM else 1, c]
        if d in (XM, XP):
            return px[d - XM, c, j]
        inner = (d == YP) == (c == 0)
        return p_v[1 - c, j] if inner else py[d - YM, j]

    def dot(a, b):
        return jnp.dot(a, b, preferred_element_type=F32)

    eye = lax.broadcasted_iota(jnp.int32, (N, N), 0) == lax.broadcasted_iota(
        jnp.int32, (N, N), 1
    )

    def row_sums(block):
        total = jnp.sum(block, axis=1, keepdims=True)
        return jnp.sum(jnp.where(eye, total, 0.0), axis=0, keepdims=True)

    p_copy.wait()
    flipped = [[p_v[c, j].T for j in (0, 1)] for c in (0, 1)]

    def piece(c, j, d):
        block = a_v[c, j, where[c][j][d]]
        result = dot(flipped[c][j], dot(block, near(c, j, d)).astype(BF16))
        t = 2 * c + j
        pieces[t, d] = result
        return result

    INNER_Z = (ZP, ZM)
    OUTER_Z = (ZM, ZP)
    for c in (0, 1):
        for j in (0, 1):
            t = 2 * c + j
            inner_y = YP if c == 0 else YM
            y = piece(c, j, SELF) * vector(c, j, SELF)
            y += piece(c, j, INNER_Z[j]) * vector(c, j, INNER_Z[j])
            lateral = piece(c, j, inner_y)
            acc_y[t] = y + lateral * vector(c, j, inner_y)
            acc_a[t] = jnp.abs(lateral)

    sends[0].wait_recv()
    sends[1].wait_recv()
    for c in (0, 1):
        for j in (0, 1):
            t = 2 * c + j
            acc_y[t] += piece(c, j, OUTER_Z[j]) * vector(c, j, OUTER_Z[j])

    sends[6].wait_recv()
    sends[7].wait_recv()
    for c in (0, 1):
        j = 1 - c
        other = pz[1 - c, c]
        mid_self = dot(partner[c, 0], other).astype(BF16)
        mid_outer = dot(partner[c, 1], p_v[c, j]).astype(BF16)
        turned = other.T
        far = dot(turned, mid_self) + dot(turned, mid_outer)
        t = 2 * c + j
        split = pieces[t, SELF] + pieces[t, OUTER_Z[j]] + far
        whole = (pieces[2 * c, SELF] + pieces[2 * c, ZP]) + (
            pieces[2 * c + 1, SELF] + pieces[2 * c + 1, ZM]
        )
        acc_a[t] += jnp.abs(jnp.where(phase[c] == 1, split, whole))
        for i in (0, 1):
            t = 2 * c + i
            acc_a[t] += jnp.abs(
                jnp.where(phase[c] == 1, pieces[t, INNER_Z[i]], pieces[t, OUTER_Z[i]])
            )

    sends[4].wait_recv()
    sends[5].wait_recv()
    for c in (0, 1):
        d = YM if c == 0 else YP
        for j in (0, 1):
            t = 2 * c + j
            lateral = piece(c, j, d)
            acc_y[t] += lateral * vector(c, j, d)
            acc_a[t] += jnp.abs(lateral)

    sends[2].wait_recv()
    sends[3].wait_recv()
    sums, scales = [], []
    for c in (0, 1):
        for j in (0, 1):
            t = 2 * c + j
            low, high = piece(c, j, XM), piece(c, j, XP)
            sums.append(row_sums(acc_y[t] + low * vector(c, j, XM) + high * vector(c, j, XP)))
            scales.append(row_sums(acc_a[t] + jnp.abs(low) + jnp.abs(high)))

    rhs = rhs_ref[0, :, 0, :]

    def parts(c, lower, upper, extra):
        whole = extra + lower + upper
        split = phase[c] == 1
        return jnp.where(split, lower, whole), jnp.where(split, extra + upper, whole)

    def defects(c, sums):
        return parts(c, -sums[2 * c], -sums[2 * c + 1], rhs[c : c + 1])

    def put(full, swapped, base, pair):
        full[base : base + 1, :] = pair[0]
        full[base + 1 : base + 2, :] = pair[1]
        swapped[base : base + 1, :] = pair[1]
        swapped[base + 1 : base + 2, :] = pair[0]

    def exchange(k, full, swapped, target):
        copies = [
            pltpu.make_async_remote_copy(
                full if r < 4 else swapped, target.at[opposite(r)],
                small_send.at[k], small_recv.at[k],
                device_id=devices[r], device_id_type=MESH,
            )
            for r in range(14)
        ]
        for copy in copies:
            copy.start()
        pltpu.make_async_copy(target, target, small_recv.at[k]).wait()

    def combined(full, target, even, straddle):
        crossing = jnp.where(even, target[4], target[5])
        own = full[...]
        own = own + jnp.where(straddle, crossing, 0.0)
        out = [own, jnp.where(straddle, own, crossing)]
        for l in range(4):
            far = jnp.where(even, target[6 + 2 * l], target[7 + 2 * l])
            moved = r0[START_FROM.index(l), 1, 0 : even.shape[0]] > 0.5
            out.append(target[l] + jnp.where(moved, far, 0.0))
        return out

    for c in (0, 1):
        put(f1, s1, 2 * c, defects(c, sums))
        put(f1, s1, 4 + 2 * c, parts(c, scales[2 * c], scales[2 * c + 1], EPSILON))
    exchange(1, f1, s1, r1)
    for k, total in enumerate(combined(f1, r1, even8, straddle8)):
        inverse = 1.0 / total[4:8]
        inv_ref[k, 0:4] = inverse
        w_ref[k, 0:4] = w_ref[k, 0:4] + total[0:4] * inverse

    def apply_coarse():
        out = []
        for c in (0, 1):
            for j in (0, 1):
                t = 2 * c + j
                acc = pieces[t, 0] * vector(c, j, 0)
                for d in range(1, 7):
                    acc += pieces[t, d] * vector(c, j, d)
                out.append(row_sums(acc))
        return out

    sums = apply_coarse()
    for c in (0, 1):
        put(f2, s2, 2 * c, defects(c, sums))
    exchange(2, f2, s2, r2)
    for k, total in enumerate(combined(f2, r2, even4, straddle4)):
        w_ref[k, 0:4] = w_ref[k, 0:4] + total * inv_ref[k, 0:4]

    sums = apply_coarse()
    last = [defects(c, sums) for c in (0, 1)]
    for c in (0, 1):
        s3[c : c + 1, :] = last[c][0]
    down = pltpu.make_async_remote_copy(
        s3, r3, small_send.at[3], small_recv.at[3], device_id=devices[4], device_id_type=MESH
    )
    down.start()
    for c in (0, 1):
        sol_ref[0, c, :, :] = w_ref[OWN, 2 * c + 1 : 2 * c + 2, :]
    down.wait_recv()
    for c in (0, 1):
        res_ref[0, c, :, :] = last[c][1] + jnp.where(phase[c] == 1, r3[c : c + 1, :], 0.0)

    down.wait_send()
    pltpu.make_async_copy(r0, r0, small_send.at[0]).wait()
    pltpu.make_async_copy(r1, r1, small_send.at[1]).wait()
    pltpu.make_async_copy(r2, r2, small_send.at[2]).wait()
    for copy in sends:
        copy.wait_send()


def body(a_blocks, a_cols, p_blocks, agg_ids, coarse_cols, coarse_rhs, coarse_start):
    del coarse_cols
    vmem = pl.BlockSpec(memory_space=pltpu.VMEM)
    smem = pl.BlockSpec(memory_space=pltpu.SMEM)
    hbm = pl.BlockSpec(memory_space=pl.ANY)
    shape = jax.ShapeDtypeStruct(coarse_rhs.shape, F32)
    return pl.pallas_call(
        kernel,
        out_shape=(shape, shape),
        in_specs=[hbm, smem, hbm, smem, vmem, vmem],
        out_specs=(vmem, vmem),
        scratch_shapes=[
            pltpu.VMEM((2, 2, 7, N, N), BF16),
            pltpu.VMEM((2, 2, N, N), BF16),
            pltpu.VMEM((2, 2, 2, N, N), BF16),
            pltpu.VMEM((2, 2, N, N), BF16),
            pltpu.VMEM((2, 2, N, N), BF16),
            pltpu.VMEM((2, 2, N, N), BF16),
            pltpu.VMEM((2, 2, N, N), BF16),
            pltpu.VMEM((4, 7, N, N), F32),
            pltpu.VMEM((4, N, N), F32),
            pltpu.VMEM((4, N, N), F32),
            pltpu.VMEM((6, 8, N), F32),
            pltpu.VMEM((2, 8, N), F32),
            pltpu.VMEM((10, 2, 8, N), F32),
            pltpu.VMEM((8, N), F32),
            pltpu.VMEM((8, N), F32),
            pltpu.VMEM((14, 8, N), F32),
            pltpu.VMEM((6, 8, N), F32),
            pltpu.VMEM((4, N), F32),
            pltpu.VMEM((4, N), F32),
            pltpu.VMEM((14, 4, N), F32),
            pltpu.VMEM((2, N), F32),
            pltpu.VMEM((2, N), F32),
            pltpu.SemaphoreType.DMA,
            pltpu.SemaphoreType.DMA,
            pltpu.SemaphoreType.DMA((8,)),
            pltpu.SemaphoreType.DMA((8,)),
            pltpu.SemaphoreType.DMA((4,)),
            pltpu.SemaphoreType.DMA((4,)),
        ],
        compiler_params=pltpu.CompilerParams(
            collective_id=0, has_side_effects=True, vmem_limit_bytes=32 * 2**20
        ),
        name="coarse_setup",
    )(a_blocks, a_cols, p_blocks, agg_ids, coarse_rhs, coarse_start)


def solution(mesh):
    return jax.shard_map(
        body,
        mesh=mesh,
        in_specs=(
            P("gx", "gy", "gz", None, None, None),
            P("gx", "gy", "gz", None),
            P("gx", "gy", "gz", None, None),
            P("gx", "gy", "gz"),
            P("gx", "gy", "gz", None),
            P("gx", "gy", "gz", None),
            P("gx", "gy", "gz", None),
        ),
        out_specs=(P("gx", "gy", "gz", None), P("gx", "gy", "gz", None)),
        check_vma=False,
    )
```

time: 158 us -> 37.9 us (0.24)
  starting transfers between devices: 73.7 us -> 0 us
  waiting for transfers between devices: 41.6 us -> 0 us
  Pallas kernels: 0 us -> 31.1 us
  local copies, waits for them, and re-layouts: 21.5 us -> 5.92 us
  matrix products: 14.1 us -> 0 us
  other arithmetic: 4.45 us -> 0 us
    ppermute x25 -> x0, starting transfers between devices: 73.7 us -> none  [the longest x12 35.3 us: extended(): lax.ppermute(lax.slice_in_dim(block, 0, width, axis=dim), axis, backward)]
    ppermute x25 -> x0, waiting for transfers between devices: 41.6 us -> none  [the longest x12 22.8 us: extended(): lax.ppermute(lax.slice_in_dim(block, block.shape[dim] - width, None, axis...]
    pallas_call x0 -> x1, Pallas kernels: none -> 31.1 us  [body(): pl.pallas_call(kernel, out_shape=(shape, shape), in_specs=[hbm, smem, hbm...]
    dot_general x6 -> x0, matrix products: 14.1 us -> none  [the longest x3 4.79 us: apply_coarse(): jnp.einsum('abcsij,abcsj->abci', operator, picked, precision=lax.Precisio...]
    another operation x8 -> x0, local copies, waits for them, and re-layouts: 9.52 us -> none
    gather x6 -> x0, local copies, waits for them, and re-layouts: 8.46 us -> none  [the longest x2 5.15 us: body(): arrived = shifted(pieces[:, :, 0][row_x, row_y, order], 'gz', -1)]
    unnamed x16 -> x14, local copies, waits for them, and re-layouts: 1.72 us -> 5.92 us
  transfers between devices with their start and end apart: 25 -> 0, of which waited for: 16 -> 0; matrix products, arithmetic and copies ran while one was open for 8% -> 0% of each run, Pallas kernels for 0% -> 0%
where the time goes in v1:
time: 37.9 us; the launch traced here: 37.7 us
  Pallas kernels  31.1 us (82%)
  local copies, waits for them, and re-layouts  5.92 us (16%)
  between operations  0.65 us (2%)
    pallas_call x1, Pallas kernels, body(): pl.pallas_call(kernel, out_shape=(shape, shape), in_specs=[hbm, smem, hbm...  31.1 us
    unnamed x14, local copies, waits for them, and re-layouts  5.92 us

profile of v1, /device:TPU:1, one launch (start us, length us, event | category | flops | bytes accessed | tf_op | source)
XLA Modules:
  0.0 37.7 jit_solution(5388163497253775373)
XLA Ops:
  0.6 0.0 copy-start
  0.6 1.2 %copy-done = bf16[1,2,2,7,128,128]{5,4,3,2,1,0:T(8,128)(2,1)S(1)} copy-done((bf16[1,2,2,7,128,128]{5,4,3,2,1,0:T(8,128)(2,1)S(1)}, bf16[1,2,2,7,128,128]{5,4,3,2,1,0:T(8,128)(2,1)}, u32[]{:S(2)}) %copy-start) | copy-done | bytes 917528
  1.8 0.0 copy-start.1
  1.8 0.9 %copy-done.1 = bf16[1,2,2,128,128]{4,3,2,1,0:T(8,128)(2,1)S(1)} copy-done((bf16[1,2,2,128,128]{4,3,2,1,0:T(8,128)(2,1)S(1)}, bf16[1,2,2,128,128]{4,3,2,1,0:T(8,128)(2,1)}, u32[]{:S(2)}) %copy-start.1) | copy-done | bytes 131096
  2.7 0.0 copy-start.2
  2.7 0.7 %copy-done.2 = s32[1,2,2,7]{3,2,1,0:T(2,128)S(1)} copy-done((s32[1,2,2,7]{3,2,1,0:T(2,128)S(1)}, s32[1,2,2,7]{3,2,1,0:T(2,128)}, u32[]{:S(2)}) %copy-start.2) | copy-done | bytes 136
  3.4 0.0 copy-start.3
  3.4 0.7 %copy-done.3 = s32[1,2,2]{2,1,0:T(2,128)S(1)} copy-done((s32[1,2,2]{2,1,0:T(2,128)S(1)}, s32[1,2,2]{2,1,0:T(2,128)}, u32[]{:S(2)}) %copy-start.3) | copy-done | bytes 40
  4.1 0.0 copy-start.4
  4.1 0.7 %copy-done.4 = f32[1,2,1,128]{3,2,1,0:T(1,128)S(1)} copy-done((f32[1,2,1,128]{3,2,1,0:T(1,128)S(1)}, f32[1,2,1,128]{3,2,1,0:T(1,128)}, u32[]{:S(2)}) %copy-start.4) | copy-done | bytes 1048
  4.8 0.0 copy-start.5
  4.8 0.7 %copy-done.5 = f32[1,2,1,128]{3,2,1,0:T(1,128)S(1)} copy-done((f32[1,2,1,128]{3,2,1,0:T(1,128)S(1)}, f32[1,2,1,128]{3,2,1,0:T(1,128)}, u32[]{:S(2)}) %copy-start.5) | copy-done | bytes 1048
  5.4 31.1 %coarse_setup.1 = (f32[1,2,1,128]{3,2,1,0:T(1,128)S(1)}, f32[1,2,1,128]{3,2,1,0:T(1,128)S(1)}) custom-call(bf16[1,2,2,7,128,128]{5,4,3,2,1,0:T(8,128)(2,1)S(1)} %copy-done, s32[1,2,2,7]{3,2,1,0:T(2,128)S(1)} %copy-done.2, bf16[1,2,2,128,128]{4,3,2,1,0:T(8,128)(2,1)S(1)} %copy-done.1, s32[1,2,2]{2,1,0:T(2,128)S(1)} %copy-done.3, ...), custom_call_target="tpu_custom_call" | custom-call | tf_op jit(solution)/shard_map/coarse_setup/pallas_call | solution.py:345
  36.5 0.6 %copy.10 = f32[1,2,1,128]{3,2,1,0:T(1,128)} copy(f32[1,2,1,128]{3,2,1,0:T(1,128)S(1)} %get-tuple-element.4) | data formatting | bytes 2048
  37.1 0.6 %copy.11 = f32[1,2,1,128]{3,2,1,0:T(1,128)} copy(f32[1,2,1,128]{3,2,1,0:T(1,128)S(1)} %get-tuple-element.5) | data formatting | bytes 2048
Async XLA Ops:
  0.6 1.2 %copy-start = (bf16[1,2,2,7,128,128]{5,4,3,2,1,0:T(8,128)(2,1)S(1)}, bf16[1,2,2,7,128,128]{5,4,3,2,1,0:T(8,128)(2,1)}, u32[]{:S(2)}) copy-start(bf16[1,2,2,7,128,128]{5,4,3,2,1,0:T(8,128)(2,1)} %a_hbm.1) | copy-start | bytes 2752516
  1.8 0.9 %copy-start.1 = (bf16[1,2,2,128,128]{4,3,2,1,0:T(8,128)(2,1)S(1)}, bf16[1,2,2,128,128]{4,3,2,1,0:T(8,128)(2,1)}, u32[]{:S(2)}) copy-start(bf16[1,2,2,128,128]{4,3,2,1,0:T(8,128)(2,1)} %p_hbm.1) | copy-start | bytes 393220
  2.7 0.7 %copy-start.2 = (s32[1,2,2,7]{3,2,1,0:T(2,128)S(1)}, s32[1,2,2,7]{3,2,1,0:T(2,128)}, u32[]{:S(2)}) copy-start(s32[1,2,2,7]{3,2,1,0:T(2,128)} %cols_ref.1) | copy-start | bytes 340
  3.4 0.7 %copy-start.3 = (s32[1,2,2]{2,1,0:T(2,128)S(1)}, s32[1,2,2]{2,1,0:T(2,128)}, u32[]{:S(2)}) copy-start(s32[1,2,2]{2,1,0:T(2,128)} %agg_ref.1) | copy-start | bytes 52
  4.1 0.7 %copy-start.4 = (f32[1,2,1,128]{3,2,1,0:T(1,128)S(1)}, f32[1,2,1,128]{3,2,1,0:T(1,128)}, u32[]{:S(2)}) copy-start(f32[1,2,1,128]{3,2,1,0:T(1,128)} %rhs_ref.1) | copy-start | bytes 3076
  4.8 0.7 %copy-start.5 = (f32[1,2,1,128]{3,2,1,0:T(1,128)S(1)}, f32[1,2,1,128]{3,2,1,0:T(1,128)}, u32[]{:S(2)}) copy-start(f32[1,2,1,128]{3,2,1,0:T(1,128)} %start_ref.1) | copy-start | bytes 3076

commit v2 on v1

--- a/solution.py
+++ b/solution.py
@@ -29,11 +29,12 @@
 
 
 def kernel(
-    a_hbm, cols_ref, p_hbm, agg_ref, rhs_ref, start_ref,
-    sol_ref, res_ref,
+    a_hbm, cols_hbm, p_hbm, agg_hbm, rhs_hbm, start_hbm,
+    out_ref,
+    cols_ref, agg_ref, rhs_ref, start_ref,
     a_v, p_v, px, py, pz, stage, partner, pieces, acc_y, acc_a,
     w_ref, m0, r0, f1, s1, r1, inv_ref, f2, s2, r2, s3, r3,
-    a_sem, p_sem, bulk_send, bulk_recv, small_send, small_recv,
+    a_sem, p_sem, in_sem, bulk_send, bulk_recv, small_send, small_recv,
 ):
     gx, gy, gz = lax.axis_index("gx"), lax.axis_index("gy"), lax.axis_index("gz")
     nx, ny, nz = lax.axis_size("gx"), lax.axis_size("gy"), lax.axis_size("gz")
@@ -52,10 +53,21 @@
     for r in range(14):
         pl.semaphore_signal(barrier, inc=1, device_id=devices[r], device_id_type=MESH)
 
+    inputs = [
+        pltpu.make_async_copy(source, target, in_sem.at[k])
+        for k, (source, target) in enumerate(
+            ((agg_hbm, agg_ref), (start_hbm, start_ref), (cols_hbm, cols_ref), (rhs_hbm, rhs_ref))
+        )
+    ]
+    for copy in inputs:
+        copy.start()
     p_copy = pltpu.make_async_copy(p_hbm.at[0], p_v, p_sem)
     p_copy.start()
     a_copy = pltpu.make_async_copy(a_hbm.at[0], a_v, a_sem)
     a_copy.start()
+
+    for copy in inputs:
+        copy.wait()
 
     phase = [
         (agg_ref[0, c, 0] != (gx * total_y + 2 * gy + c) * nz + gz).astype(jnp.int32)
@@ -323,10 +335,10 @@
     )
     down.start()
     for c in (0, 1):
-        sol_ref[0, c, :, :] = w_ref[OWN, 2 * c + 1 : 2 * c + 2, :]
+        out_ref[0, c, 0:1, :] = w_ref[OWN, 2 * c + 1 : 2 * c + 2, :]
     down.wait_recv()
     for c in (0, 1):
-        res_ref[0, c, :, :] = last[c][1] + jnp.where(phase[c] == 1, r3[c : c + 1, :], 0.0)
+        out_ref[0, c, 1:2, :] = last[c][1] + jnp.where(phase[c] == 1, r3[c : c + 1, :], 0.0)
 
     down.wait_send()
     pltpu.make_async_copy(r0, r0, small_send.at[0]).wait()
@@ -339,15 +351,18 @@
 def body(a_blocks, a_cols, p_blocks, agg_ids, coarse_cols, coarse_rhs, coarse_start):
     del coarse_cols
     vmem = pl.BlockSpec(memory_space=pltpu.VMEM)
-    smem = pl.BlockSpec(memory_space=pltpu.SMEM)
-    hbm = pl.BlockSpec(memory_space=pl.ANY)
-    shape = jax.ShapeDtypeStruct(coarse_rhs.shape, F32)
-    return pl.pallas_call(
+    hbm = pl.BlockSpec(memory_space=pltpu.HBM)
+    one, rows, layers, width = coarse_rhs.shape
+    out = pl.pallas_call(
         kernel,
-        out_shape=(shape, shape),
-        in_specs=[hbm, smem, hbm, smem, vmem, vmem],
-        out_specs=(vmem, vmem),
+        out_shape=jax.ShapeDtypeStruct((one, rows, 2 * layers, width), F32),
+        in_specs=[hbm] * 6,
+        out_specs=vmem,
         scratch_shapes=[
+            pltpu.SMEM(a_cols.shape, jnp.int32),
+            pltpu.SMEM(agg_ids.shape, jnp.int32),
+            pltpu.VMEM(coarse_rhs.shape, F32),
+            pltpu.VMEM(coarse_start.shape, F32),
             pltpu.VMEM((2, 2, 7, N, N), BF16),
             pltpu.VMEM((2, 2, N, N), BF16),
             pltpu.VMEM((2, 2, 2, N, N), BF16),
@@ -372,16 +387,18 @@
             pltpu.VMEM((2, N), F32),
             pltpu.SemaphoreType.DMA,
             pltpu.SemaphoreType.DMA,
+            pltpu.SemaphoreType.DMA((4,)),
             pltpu.SemaphoreType.DMA((8,)),
             pltpu.SemaphoreType.DMA((8,)),
             pltpu.SemaphoreType.DMA((4,)),
             pltpu.SemaphoreType.DMA((4,)),
         ],
         compiler_params=pltpu.CompilerParams(
-            collective_id=0, has_side_effects=True, vmem_limit_bytes=32 * 2**20
+            collective_id=0, has_side_effects=True, vmem_limit_bytes=63 * 2**20
         ),
         name="coarse_setup",
     )(a_blocks, a_cols, p_blocks, agg_ids, coarse_rhs, coarse_start)
+    return out[:, :, 0:1], out[:, :, 1:2]
 
 
 def solution(mesh):

time: 37.9 us -> 33.4 us (0.88)
  local copies, waits for them, and re-layouts: 5.92 us -> 1.32 us
    unnamed x14 -> x0, local copies, waits for them, and re-layouts: 5.92 us -> none
    slice x0 -> x1, local copies, waits for them, and re-layouts: none -> 1.32 us  [body(): return (out[:, :, 0:1], out[:, :, 1:2])]
where the time goes in v2:
time: 33.4 us; the launch traced here: 33.2 us
  Pallas kernels  31.3 us (94%)
  local copies, waits for them, and re-layouts  1.32 us (4%)
  between operations  0.64 us (2%)
    pallas_call x1, Pallas kernels, body(): pl.pallas_call(kernel, out_shape=jax.ShapeDtypeStruct((one, rows, 2 * lay...  31.3 us
    slice x1, local copies, waits for them, and re-layouts, body(): return (out[:, :, 0:1], out[:, :, 1:2])  1.32 us

profile of v2, /device:TPU:1, one launch (start us, length us, event | category | flops | bytes accessed | tf_op | source)
XLA Modules:
  0.0 33.2 jit_solution(13057191287926434384)
XLA Ops:
  0.6 31.3 %coarse_setup.1 = f32[1,2,2,128]{3,2,1,0:T(2,128)} custom-call(bf16[1,2,2,7,128,128]{5,4,3,2,1,0:T(8,128)(2,1)} %a_hbm.1, s32[1,2,2,7]{3,2,1,0:T(2,128)} %cols_hbm.1, bf16[1,2,2,128,128]{4,3,2,1,0:T(8,128)(2,1)} %p_hbm.1, s32[1,2,2]{2,1,0:T(2,128)} %agg_hbm.1, f32[1,2,1,128]{3,2,1,0:T(1,128)} %rhs_hbm.1, f32[1,2,1,128]{3,2,1,0:T(1,128)} %start_hbm.1), custom_call_target="tpu_custom_call" | custom-call | tf_op jit(solution)/shard_map/coarse_setup/pallas_call | solution.py:356
  31.9 1.3 %fusion = (f32[1,2,1,128]{3,2,1,0:T(1,128)}, f32[1,2,1,128]{3,2,1,0:T(1,128)}) fusion(f32[1,2,2,128]{3,2,1,0:T(2,128)} %coarse_setup.1), kind=kLoop, calls=%fused_computation | loop fusion | bytes 4096 | tf_op jit(solution)/shard_map/slice | solution.py:401

commit v3 on v2

--- a/solution.py
+++ b/solution.py
@@ -24,17 +24,18 @@
     return RELATIONS.index(tuple(-d for d in RELATIONS[r]))
 
 
-START_TO = [0, 1, 2, 3, 4, 5, 7, 9, 11, 13]
-START_FROM = [opposite(r) for r in START_TO]
+FACES = range(6)
+UPWARD = (7, 9, 11, 13)
+ORDER = list(range(6, 14)) + [4, 5, 0, 1, 2, 3]
 
 
 def kernel(
     a_hbm, cols_hbm, p_hbm, agg_hbm, rhs_hbm, start_hbm,
     out_ref,
     cols_ref, agg_ref, rhs_ref, start_ref,
-    a_v, p_v, px, py, pz, stage, partner, pieces, acc_y, acc_a,
-    w_ref, m0, r0, f1, s1, r1, inv_ref, f2, s2, r2, s3, r3,
-    a_sem, p_sem, in_sem, bulk_send, bulk_recv, small_send, small_recv,
+    a_v, p_v, px, py, pz, stage, partner, pieces, acc_a,
+    w_ref, m0, r0, d0, f1, s1, r1, inv_ref, f2, s2, r2, s3, r3,
+    a_sem, p_sem, in_sem, bulk_send, bulk_recv, small_send, small_recv, far_send, far_recv,
 ):
     gx, gy, gz = lax.axis_index("gx"), lax.axis_index("gy"), lax.axis_index("gz")
     nx, ny, nz = lax.axis_size("gx"), lax.axis_size("gy"), lax.axis_size("gz")
@@ -50,7 +51,7 @@
 
     devices = [device(r) for r in range(14)]
     barrier = pltpu.get_barrier_semaphore()
-    for r in range(14):
+    for r in (6, 8, 10, 12, *FACES):
         pl.semaphore_signal(barrier, inc=1, device_id=devices[r], device_id_type=MESH)
 
     inputs = [
@@ -101,16 +102,23 @@
     m0[0, 4:8, :] = jnp.zeros((4, N), F32)
     m0[1] = ph8
 
-    pl.semaphore_wait(barrier, 14)
-
-    small = [
+    where = [[[place(c, j, d) for d in range(7)] for j in (0, 1)] for c in (0, 1)]
+    a_copy.wait()
+    stage[0, 0] = a_v[0, 0, where[0][0][SELF]]
+    stage[0, 1] = a_v[0, 0, where[0][0][ZM]]
+    stage[1, 0] = a_v[1, 1, where[1][1][SELF]]
+    stage[1, 1] = a_v[1, 1, where[1][1][ZP]]
+
+    pl.semaphore_wait(barrier, len(FACES) + len(UPWARD))
+
+    far_starts = [
         pltpu.make_async_remote_copy(
-            m0, r0.at[START_FROM.index(opposite(r))], small_send.at[0], small_recv.at[0],
+            m0, d0.at[opposite(r) // 2 - 3], far_send, far_recv,
             device_id=devices[r], device_id_type=MESH,
         )
-        for r in START_TO
+        for r in UPWARD
     ]
-    for copy in small:
+    for copy in far_starts:
         copy.start()
 
     def bulk(k, source, target, r):
@@ -129,29 +137,17 @@
         bulk(6, stage.at[0], partner.at[0], 4),
         bulk(7, stage.at[1], partner.at[1], 5),
     ]
-    for copy in sends[:6]:
+    near_starts = [
+        pltpu.make_async_remote_copy(
+            m0, r0.at[opposite(r)], small_send.at[0], small_recv.at[0],
+            device_id=devices[r], device_id_type=MESH,
+        )
+        for r in FACES
+    ]
+    for k in (2, 3, 0, 1, 6, 7, 4, 5):
+        sends[k].start()
+    for copy in near_starts:
         copy.start()
-
-    where = [[[place(c, j, d) for d in range(7)] for j in (0, 1)] for c in (0, 1)]
-
-    a_copy.wait()
-    stage[0, 0] = a_v[0, 0, where[0][0][SELF]]
-    stage[0, 1] = a_v[0, 0, where[0][0][ZM]]
-    stage[1, 0] = a_v[1, 1, where[1][1][SELF]]
-    stage[1, 1] = a_v[1, 1, where[1][1][ZP]]
-    sends[6].start()
-    sends[7].start()
-
-    pltpu.make_async_copy(r0, r0, small_recv.at[0]).wait()
-    below, above = r0[START_FROM.index(4), 0, 0:4], r0[START_FROM.index(5), 0, 0:4]
-    mine = m0[0, 0:4]
-    w_ref[OWN, 0:4] = jnp.where(straddle4 & even4, below, mine)
-    w_ref[ZED, 0:4] = jnp.where(even4, below, jnp.where(straddle4, mine, above))
-    for l in range(4):
-        side = START_FROM.index(l)
-        far = START_FROM.index(6 + 2 * l)
-        moved = (r0[side, 1, 0:4] > 0.5) & even4
-        w_ref[2 + l, 0:4] = jnp.where(moved, r0[far, 0, 0:4], r0[side, 0, 0:4])
 
     def vector(c, j, d):
         t = 2 * c + j
@@ -203,20 +199,22 @@
     OUTER_Z = (ZM, ZP)
     for c in (0, 1):
         for j in (0, 1):
-            t = 2 * c + j
-            inner_y = YP if c == 0 else YM
-            y = piece(c, j, SELF) * vector(c, j, SELF)
-            y += piece(c, j, INNER_Z[j]) * vector(c, j, INNER_Z[j])
-            lateral = piece(c, j, inner_y)
-            acc_y[t] = y + lateral * vector(c, j, inner_y)
-            acc_a[t] = jnp.abs(lateral)
+            piece(c, j, SELF)
+            piece(c, j, INNER_Z[j])
+            acc_a[2 * c + j] = jnp.abs(piece(c, j, YP if c == 0 else YM))
+
+    sends[4].wait_recv()
+    sends[5].wait_recv()
+    for c in (0, 1):
+        d = YM if c == 0 else YP
+        for j in (0, 1):
+            acc_a[2 * c + j] += jnp.abs(piece(c, j, d))
 
     sends[0].wait_recv()
     sends[1].wait_recv()
     for c in (0, 1):
         for j in (0, 1):
-            t = 2 * c + j
-            acc_y[t] += piece(c, j, OUTER_Z[j]) * vector(c, j, OUTER_Z[j])
+            piece(c, j, OUTER_Z[j])
 
     sends[6].wait_recv()
     sends[7].wait_recv()
@@ -239,74 +237,24 @@
                 jnp.where(phase[c] == 1, pieces[t, INNER_Z[i]], pieces[t, OUTER_Z[i]])
             )
 
-    sends[4].wait_recv()
-    sends[5].wait_recv()
-    for c in (0, 1):
-        d = YM if c == 0 else YP
-        for j in (0, 1):
-            t = 2 * c + j
-            lateral = piece(c, j, d)
-            acc_y[t] += lateral * vector(c, j, d)
-            acc_a[t] += jnp.abs(lateral)
-
     sends[2].wait_recv()
     sends[3].wait_recv()
-    sums, scales = [], []
+    scales = []
     for c in (0, 1):
         for j in (0, 1):
             t = 2 * c + j
             low, high = piece(c, j, XM), piece(c, j, XP)
-            sums.append(row_sums(acc_y[t] + low * vector(c, j, XM) + high * vector(c, j, XP)))
             scales.append(row_sums(acc_a[t] + jnp.abs(low) + jnp.abs(high)))
 
-    rhs = rhs_ref[0, :, 0, :]
-
-    def parts(c, lower, upper, extra):
-        whole = extra + lower + upper
-        split = phase[c] == 1
-        return jnp.where(split, lower, whole), jnp.where(split, extra + upper, whole)
-
-    def defects(c, sums):
-        return parts(c, -sums[2 * c], -sums[2 * c + 1], rhs[c : c + 1])
-
-    def put(full, swapped, base, pair):
-        full[base : base + 1, :] = pair[0]
-        full[base + 1 : base + 2, :] = pair[1]
-        swapped[base : base + 1, :] = pair[1]
-        swapped[base + 1 : base + 2, :] = pair[0]
-
-    def exchange(k, full, swapped, target):
-        copies = [
-            pltpu.make_async_remote_copy(
-                full if r < 4 else swapped, target.at[opposite(r)],
-                small_send.at[k], small_recv.at[k],
-                device_id=devices[r], device_id_type=MESH,
-            )
-            for r in range(14)
-        ]
-        for copy in copies:
-            copy.start()
-        pltpu.make_async_copy(target, target, small_recv.at[k]).wait()
-
-    def combined(full, target, even, straddle):
-        crossing = jnp.where(even, target[4], target[5])
-        own = full[...]
-        own = own + jnp.where(straddle, crossing, 0.0)
-        out = [own, jnp.where(straddle, own, crossing)]
-        for l in range(4):
-            far = jnp.where(even, target[6 + 2 * l], target[7 + 2 * l])
-            moved = r0[START_FROM.index(l), 1, 0 : even.shape[0]] > 0.5
-            out.append(target[l] + jnp.where(moved, far, 0.0))
-        return out
-
-    for c in (0, 1):
-        put(f1, s1, 2 * c, defects(c, sums))
-        put(f1, s1, 4 + 2 * c, parts(c, scales[2 * c], scales[2 * c + 1], EPSILON))
-    exchange(1, f1, s1, r1)
-    for k, total in enumerate(combined(f1, r1, even8, straddle8)):
-        inverse = 1.0 / total[4:8]
-        inv_ref[k, 0:4] = inverse
-        w_ref[k, 0:4] = w_ref[k, 0:4] + total[0:4] * inverse
+    pltpu.make_async_copy(r0, r0, small_recv.at[0]).wait()
+    below, above = r0[4, 0, 0:4], r0[5, 0, 0:4]
+    mine = m0[0, 0:4]
+    w_ref[OWN, 0:4] = jnp.where(straddle4 & even4, below, mine)
+    w_ref[ZED, 0:4] = jnp.where(even4, below, jnp.where(straddle4, mine, above))
+    pltpu.make_async_copy(d0, d0, far_recv).wait()
+    for l in range(4):
+        moved = (r0[l, 1, 0:4] > 0.5) & even4
+        w_ref[2 + l, 0:4] = jnp.where(moved, d0[l, 0, 0:4], r0[l, 0, 0:4])
 
     def apply_coarse():
         out = []
@@ -320,6 +268,56 @@
         return out
 
     sums = apply_coarse()
+    rhs = rhs_ref[0, :, 0, :]
+
+    def parts(c, lower, upper, extra):
+        whole = extra + lower + upper
+        split = phase[c] == 1
+        return jnp.where(split, lower, whole), jnp.where(split, extra + upper, whole)
+
+    def defects(c, sums):
+        return parts(c, -sums[2 * c], -sums[2 * c + 1], rhs[c : c + 1])
+
+    def put(full, swapped, base, pair):
+        full[base : base + 1, :] = pair[0]
+        full[base + 1 : base + 2, :] = pair[1]
+        swapped[base : base + 1, :] = pair[1]
+        swapped[base + 1 : base + 2, :] = pair[0]
+
+    def exchange(k, full, swapped, target):
+        copies = [
+            pltpu.make_async_remote_copy(
+                full if r < 4 else swapped, target.at[opposite(r)],
+                small_send.at[k], small_recv.at[k],
+                device_id=devices[r], device_id_type=MESH,
+            )
+            for r in ORDER
+        ]
+        for copy in copies:
+            copy.start()
+        pltpu.make_async_copy(target, target, small_recv.at[k]).wait()
+
+    def combined(full, target, even, straddle):
+        crossing = jnp.where(even, target[4], target[5])
+        own = full[...]
+        own = own + jnp.where(straddle, crossing, 0.0)
+        out = [own, jnp.where(straddle, own, crossing)]
+        for l in range(4):
+            far = jnp.where(even, target[6 + 2 * l], target[7 + 2 * l])
+            moved = r0[l, 1, 0 : even.shape[0]] > 0.5
+            out.append(target[l] + jnp.where(moved, far, 0.0))
+        return out
+
+    for c in (0, 1):
+        put(f1, s1, 2 * c, defects(c, sums))
+        put(f1, s1, 4 + 2 * c, parts(c, scales[2 * c], scales[2 * c + 1], EPSILON))
+    exchange(1, f1, s1, r1)
+    for k, total in enumerate(combined(f1, r1, even8, straddle8)):
+        inverse = 1.0 / total[4:8]
+        inv_ref[k, 0:4] = inverse
+        w_ref[k, 0:4] = w_ref[k, 0:4] + total[0:4] * inverse
+
+    sums = apply_coarse()
     for c in (0, 1):
         put(f2, s2, 2 * c, defects(c, sums))
     exchange(2, f2, s2, r2)
@@ -342,6 +340,7 @@
 
     down.wait_send()
     pltpu.make_async_copy(r0, r0, small_send.at[0]).wait()
+    pltpu.make_async_copy(d0, d0, far_send).wait()
     pltpu.make_async_copy(r1, r1, small_send.at[1]).wait()
     pltpu.make_async_copy(r2, r2, small_send.at[2]).wait()
     for copy in sends:
@@ -372,10 +371,10 @@
             pltpu.VMEM((2, 2, N, N), BF16),
             pltpu.VMEM((4, 7, N, N), F32),
             pltpu.VMEM((4, N, N), F32),
-            pltpu.VMEM((4, N, N), F32),
             pltpu.VMEM((6, 8, N), F32),
             pltpu.VMEM((2, 8, N), F32),
-            pltpu.VMEM((10, 2, 8, N), F32),
+            pltpu.VMEM((6, 2, 8, N), F32),
+            pltpu.VMEM((4, 2, 8, N), F32),
             pltpu.VMEM((8, N), F32),
             pltpu.VMEM((8, N), F32),
             pltpu.VMEM((14, 8, N), F32),
@@ -392,6 +391,8 @@
             pltpu.SemaphoreType.DMA((8,)),
             pltpu.SemaphoreType.DMA((4,)),
             pltpu.SemaphoreType.DMA((4,)),
+            pltpu.SemaphoreType.DMA,
+            pltpu.SemaphoreType.DMA,
         ],
         compiler_params=pltpu.CompilerParams(
             collective_id=0, has_side_effects=True, vmem_limit_bytes=63 * 2**20

time: 33.4 us -> 32.4 us (0.970)
  Pallas kernels: 31.3 us -> 30.3 us
    pallas_call x1, Pallas kernels: 31.3 us -> 30.3 us  [body(): pl.pallas_call(kernel, out_shape=jax.ShapeDtypeStruct((one, rows, 2 * lay...]
where the time goes in v3:
time: 32.4 us; the launch traced here: 32.2 us
  Pallas kernels  30.3 us (94%)
  local copies, waits for them, and re-layouts  1.32 us (4%)
  between operations  0.64 us (2%)
    pallas_call x1, Pallas kernels, body(): pl.pallas_call(kernel, out_shape=jax.ShapeDtypeStruct((one, rows, 2 * lay...  30.3 us
    slice x1, local copies, waits for them, and re-layouts, body(): return (out[:, :, 0:1], out[:, :, 1:2])  1.32 us

profile of v3, /device:TPU:1, one launch (start us, length us, event | category | flops | bytes accessed | tf_op | source)
XLA Modules:
  0.0 32.2 jit_solution(5082306045048079865)
XLA Ops:
  0.6 30.3 %coarse_setup.1 = f32[1,2,2,128]{3,2,1,0:T(2,128)} custom-call(bf16[1,2,2,7,128,128]{5,4,3,2,1,0:T(8,128)(2,1)} %a_hbm.1, s32[1,2,2,7]{3,2,1,0:T(2,128)} %cols_hbm.1, bf16[1,2,2,128,128]{4,3,2,1,0:T(8,128)(2,1)} %p_hbm.1, s32[1,2,2]{2,1,0:T(2,128)} %agg_hbm.1, f32[1,2,1,128]{3,2,1,0:T(1,128)} %rhs_hbm.1, f32[1,2,1,128]{3,2,1,0:T(1,128)} %start_hbm.1), custom_call_target="tpu_custom_call" | custom-call | tf_op jit(solution)/shard_map/coarse_setup/pallas_call | solution.py:355
  30.9 1.3 %fusion = (f32[1,2,1,128]{3,2,1,0:T(1,128)}, f32[1,2,1,128]{3,2,1,0:T(1,128)}) fusion(f32[1,2,2,128]{3,2,1,0:T(2,128)} %coarse_setup.1), kind=kLoop, calls=%fused_computation | loop fusion | bytes 4096 | tf_op jit(solution)/shard_map/slice | solution.py:402

commit v4 on v3

--- a/solution.py
+++ b/solution.py
@@ -103,6 +103,7 @@
     m0[1] = ph8
 
     where = [[[place(c, j, d) for d in range(7)] for j in (0, 1)] for c in (0, 1)]
+    p_copy.wait()
     a_copy.wait()
     stage[0, 0] = a_v[0, 0, where[0][0][SELF]]
     stage[0, 1] = a_v[0, 0, where[0][0][ZM]]
@@ -111,16 +112,6 @@
 
     pl.semaphore_wait(barrier, len(FACES) + len(UPWARD))
 
-    far_starts = [
-        pltpu.make_async_remote_copy(
-            m0, d0.at[opposite(r) // 2 - 3], far_send, far_recv,
-            device_id=devices[r], device_id_type=MESH,
-        )
-        for r in UPWARD
-    ]
-    for copy in far_starts:
-        copy.start()
-
     def bulk(k, source, target, r):
         return pltpu.make_async_remote_copy(
             source, target, bulk_send.at[k], bulk_recv.at[k],
@@ -128,14 +119,16 @@
         )
 
     sends = [
-        bulk(0, p_hbm.at[0, :, 1], pz.at[0], 5),
-        bulk(1, p_hbm.at[0, :, 0], pz.at[1], 4),
-        bulk(2, p_hbm.at[0], px.at[0], 1),
-        bulk(3, p_hbm.at[0], px.at[1], 0),
-        bulk(4, p_hbm.at[0, 1], py.at[0], 3),
-        bulk(5, p_hbm.at[0, 0], py.at[1], 2),
+        bulk(0, p_v.at[0], px.at[0, 0], 1),
+        bulk(1, p_v.at[0], px.at[1, 0], 0),
+        bulk(2, p_v.at[1], px.at[0, 1], 1),
+        bulk(3, p_v.at[1], px.at[1, 1], 0),
+        bulk(4, p_v.at[:, 1], pz.at[0], 5),
+        bulk(5, p_v.at[:, 0], pz.at[1], 4),
         bulk(6, stage.at[0], partner.at[0], 4),
         bulk(7, stage.at[1], partner.at[1], 5),
+        bulk(8, p_v.at[1], py.at[0], 3),
+        bulk(9, p_v.at[0], py.at[1], 2),
     ]
     near_starts = [
         pltpu.make_async_remote_copy(
@@ -144,8 +137,15 @@
         )
         for r in FACES
     ]
-    for k in (2, 3, 0, 1, 6, 7, 4, 5):
-        sends[k].start()
+    far_starts = [
+        pltpu.make_async_remote_copy(
+            m0, d0.at[opposite(r) // 2 - 3], far_send, far_recv,
+            device_id=devices[r], device_id_type=MESH,
+        )
+        for r in UPWARD
+    ]
+    for copy in sends[:4] + far_starts + sends[4:]:
+        copy.start()
     for copy in near_starts:
         copy.start()
 
@@ -185,36 +185,36 @@
         total = jnp.sum(block, axis=1, keepdims=True)
         return jnp.sum(jnp.where(eye, total, 0.0), axis=0, keepdims=True)
 
-    p_copy.wait()
     flipped = [[p_v[c, j].T for j in (0, 1)] for c in (0, 1)]
 
-    def piece(c, j, d):
-        block = a_v[c, j, where[c][j][d]]
-        result = dot(flipped[c][j], dot(block, near(c, j, d)).astype(BF16))
-        t = 2 * c + j
-        pieces[t, d] = result
-        return result
-
-    INNER_Z = (ZP, ZM)
-    OUTER_Z = (ZM, ZP)
+    def form(c, j, *directions):
+        products = [
+            dot(a_v[c, j, where[c][j][d]], near(c, j, d)).astype(BF16) for d in directions
+        ]
+        joined = dot(flipped[c][j], jnp.concatenate(products, axis=1))
+        out = [joined[:, k * N : (k + 1) * N] for k in range(len(directions))]
+        for d, result in zip(directions, out):
+            pieces[2 * c + j, d] = result
+        return out
+
+    INNER_Z, OUTER_Z = (ZP, ZM), (ZM, ZP)
+    INNER_Y, OUTER_Y = (YP, YM), (YM, YP)
     for c in (0, 1):
         for j in (0, 1):
-            piece(c, j, SELF)
-            piece(c, j, INNER_Z[j])
-            acc_a[2 * c + j] = jnp.abs(piece(c, j, YP if c == 0 else YM))
-
-    sends[4].wait_recv()
-    sends[5].wait_recv()
-    for c in (0, 1):
-        d = YM if c == 0 else YP
+            acc_a[2 * c + j] = jnp.abs(form(c, j, SELF, INNER_Z[j], INNER_Y[c])[2])
+
+    for k in (8, 9, 4, 5):
+        sends[k].wait_recv()
+    for c in (0, 1):
         for j in (0, 1):
-            acc_a[2 * c + j] += jnp.abs(piece(c, j, d))
-
-    sends[0].wait_recv()
-    sends[1].wait_recv()
-    for c in (0, 1):
+            acc_a[2 * c + j] += jnp.abs(form(c, j, OUTER_Z[j], OUTER_Y[c])[1])
+
+    for c in (0, 1):
+        sends[2 * c].wait_recv()
+        sends[2 * c + 1].wait_recv()
         for j in (0, 1):
-            piece(c, j, OUTER_Z[j])
+            low, high = form(c, j, XM, XP)
+            acc_a[2 * c + j] += jnp.abs(low) + jnp.abs(high)
 
     sends[6].wait_recv()
     sends[7].wait_recv()
@@ -223,8 +223,10 @@
         other = pz[1 - c, c]
         mid_self = dot(partner[c, 0], other).astype(BF16)
         mid_outer = dot(partner[c, 1], p_v[c, j]).astype(BF16)
-        turned = other.T
-        far = dot(turned, mid_self) + dot(turned, mid_outer)
+        far = dot(
+            jnp.concatenate([other.T, other.T], axis=1),
+            jnp.concatenate([mid_self, mid_outer], axis=0),
+        )
         t = 2 * c + j
         split = pieces[t, SELF] + pieces[t, OUTER_Z[j]] + far
         whole = (pieces[2 * c, SELF] + pieces[2 * c, ZP]) + (
@@ -237,14 +239,7 @@
                 jnp.where(phase[c] == 1, pieces[t, INNER_Z[i]], pieces[t, OUTER_Z[i]])
             )
 
-    sends[2].wait_recv()
-    sends[3].wait_recv()
-    scales = []
-    for c in (0, 1):
-        for j in (0, 1):
-            t = 2 * c + j
-            low, high = piece(c, j, XM), piece(c, j, XP)
-            scales.append(row_sums(acc_a[t] + jnp.abs(low) + jnp.abs(high)))
+    scales = [row_sums(acc_a[t]) for t in range(4)]
 
     pltpu.make_async_copy(r0, r0, small_recv.at[0]).wait()
     below, above = r0[4, 0, 0:4], r0[5, 0, 0:4]
@@ -354,7 +349,7 @@
     one, rows, layers, width = coarse_rhs.shape
     out = pl.pallas_call(
         kernel,
-        out_shape=jax.ShapeDtypeStruct((one, rows, 2 * layers, width), F32),
+        out_shape=pltpu.VMEM((one, rows, 2 * layers, width), F32),
         in_specs=[hbm] * 6,
         out_specs=vmem,
         scratch_shapes=[
@@ -387,8 +382,8 @@
             pltpu.SemaphoreType.DMA,
             pltpu.SemaphoreType.DMA,
             pltpu.SemaphoreType.DMA((4,)),
-            pltpu.SemaphoreType.DMA((8,)),
-            pltpu.SemaphoreType.DMA((8,)),
+            pltpu.SemaphoreType.DMA((10,)),
+            pltpu.SemaphoreType.DMA((10,)),
             pltpu.SemaphoreType.DMA((4,)),
             pltpu.SemaphoreType.DMA((4,)),
             pltpu.SemaphoreType.DMA,

time: 32.4 us -> 30.9 us (0.954)
  local copies, waits for them, and re-layouts: 1.32 us -> 0.57 us
  Pallas kernels: 30.3 us -> 29.6 us
    slice x1, local copies, waits for them, and re-layouts: 1.32 us -> 0.57 us  [body(): return (out[:, :, 0:1], out[:, :, 1:2])]
    pallas_call x1, Pallas kernels: 30.3 us -> 29.6 us  [body(): pl.pallas_call(kernel, out_shape=pltpu.VMEM((one, rows, 2 * layers, width...]
where the time goes in v4:
time: 30.9 us; the launch traced here: 30.8 us
  Pallas kernels  29.6 us (96%)
  between operations  0.64 us (2%)
  local copies, waits for them, and re-layouts  0.57 us (2%)
    pallas_call x1, Pallas kernels, body(): pl.pallas_call(kernel, out_shape=pltpu.VMEM((one, rows, 2 * layers, width...  29.6 us

profile of v4, /device:TPU:1, one launch (start us, length us, event | category | flops | bytes accessed | tf_op | source)
XLA Modules:
  0.0 30.8 jit_solution(9474561856314538353)
XLA Ops:
  0.6 29.6 %coarse_setup.1 = f32[1,2,2,128]{3,2,1,0:T(2,128)S(1)} custom-call(bf16[1,2,2,7,128,128]{5,4,3,2,1,0:T(8,128)(2,1)} %a_hbm.1, s32[1,2,2,7]{3,2,1,0:T(2,128)} %cols_hbm.1, bf16[1,2,2,128,128]{4,3,2,1,0:T(8,128)(2,1)} %p_hbm.1, s32[1,2,2]{2,1,0:T(2,128)} %agg_hbm.1, f32[1,2,1,128]{3,2,1,0:T(1,128)} %rhs_hbm.1, f32[1,2,1,128]{3,2,1,0:T(1,128)} %start_hbm.1), custom_call_target="tpu_custom_call" | custom-call | tf_op jit(solution)/shard_map/coarse_setup/pallas_call | solution.py:350
  30.2 0.6 %fusion = (f32[1,2,1,128]{3,2,1,0:T(1,128)}, f32[1,2,1,128]{3,2,1,0:T(1,128)}) fusion(f32[1,2,2,128]{3,2,1,0:T(2,128)S(1)} %coarse_setup.1), kind=kLoop, calls=%fused_computation | loop fusion | bytes 4096 | tf_op jit(solution)/shard_map/slice | solution.py:397

commit v5 on v4

--- a/solution.py
+++ b/solution.py
@@ -33,9 +33,9 @@
     a_hbm, cols_hbm, p_hbm, agg_hbm, rhs_hbm, start_hbm,
     out_ref,
     cols_ref, agg_ref, rhs_ref, start_ref,
-    a_v, p_v, px, py, pz, stage, partner, pieces, acc_a,
+    a_v, p_v, px, py, pz, stage, partner, pieces, acc_a, acc_y, ahead,
     w_ref, m0, r0, d0, f1, s1, r1, inv_ref, f2, s2, r2, s3, r3,
-    a_sem, p_sem, in_sem, bulk_send, bulk_recv, small_send, small_recv, far_send, far_recv,
+    a_sem, p_sem, in_sem, bulk_send, bulk_recv, small_send, side_recv, z_recv, far_send, far_recv, last_recv,
 ):
     gx, gy, gz = lax.axis_index("gx"), lax.axis_index("gy"), lax.axis_index("gz")
     nx, ny, nz = lax.axis_size("gx"), lax.axis_size("gy"), lax.axis_size("gz")
@@ -111,6 +111,12 @@
     stage[1, 1] = a_v[1, 1, where[1][1][ZP]]
 
     pl.semaphore_wait(barrier, len(FACES) + len(UPWARD))
+
+    def arrival(k, r):
+        return (side_recv if r < 4 else z_recv if r < 6 else far_recv).at[k]
+
+    def await_arrival(buffer, semaphore):
+        pltpu.make_async_copy(buffer, buffer, semaphore).wait()
 
     def bulk(k, source, target, r):
         return pltpu.make_async_remote_copy(
@@ -132,21 +138,21 @@
     ]
     near_starts = [
         pltpu.make_async_remote_copy(
-            m0, r0.at[opposite(r)], small_send.at[0], small_recv.at[0],
+            m0, r0.at[opposite(r)], small_send.at[0], arrival(0, r),
             device_id=devices[r], device_id_type=MESH,
         )
         for r in FACES
     ]
     far_starts = [
         pltpu.make_async_remote_copy(
-            m0, d0.at[opposite(r) // 2 - 3], far_send, far_recv,
+            m0, d0.at[opposite(r) // 2 - 3], far_send, far_recv.at[0],
             device_id=devices[r], device_id_type=MESH,
         )
         for r in UPWARD
     ]
-    for copy in sends[:4] + far_starts + sends[4:]:
+    for copy in sends[:4] + far_starts + sends[4:6] + near_starts[4:] + sends[6:]:
         copy.start()
-    for copy in near_starts:
+    for copy in near_starts[:4]:
         copy.start()
 
     def vector(c, j, d):
@@ -187,6 +193,9 @@
 
     flipped = [[p_v[c, j].T for j in (0, 1)] for c in (0, 1)]
 
+    INNER_Z, OUTER_Z = (ZP, ZM), (ZM, ZP)
+    INNER_Y, OUTER_Y = (YP, YM), (YM, YP)
+
     def form(c, j, *directions):
         products = [
             dot(a_v[c, j, where[c][j][d]], near(c, j, d)).astype(BF16) for d in directions
@@ -197,24 +206,65 @@
             pieces[2 * c + j, d] = result
         return out
 
-    INNER_Z, OUTER_Z = (ZP, ZM), (ZM, ZP)
-    INNER_Y, OUTER_Y = (YP, YM), (YM, YP)
+    def outer(c, j):
+        return (OUTER_Z[j], OUTER_Y[c], XM, XP)
+
+    def prepare(c, j):
+        for k, d in enumerate(outer(c, j)):
+            left = dot(flipped[c][j], a_v[c, j, where[c][j][d]])
+            lead = left.astype(BF16)
+            ahead[2 * c + j, k, :, :N] = lead
+            ahead[2 * c + j, k, :, N:] = (left - lead.astype(F32)).astype(BF16)
+
+    def finish(c, j, d):
+        block = near(c, j, d)
+        result = dot(ahead[2 * c + j, outer(c, j).index(d)], jnp.concatenate([block, block], axis=0))
+        pieces[2 * c + j, d] = result
+        return result
+
+    def add_up(c, j, directions):
+        t = 2 * c + j
+        acc = pieces[t, directions[0]] * vector(c, j, directions[0])
+        for d in directions[1:]:
+            acc += pieces[t, d] * vector(c, j, d)
+        return acc
+
+    def apply_here():
+        for c in (0, 1):
+            for j in (0, 1):
+                acc_y[2 * c + j] = add_up(c, j, (SELF, ZM, ZP, INNER_Y[c]))
+
+    def apply_rest():
+        return [
+            row_sums(acc_y[2 * c + j] + add_up(c, j, (OUTER_Y[c], XM, XP)))
+            for c in (0, 1)
+            for j in (0, 1)
+        ]
+
     for c in (0, 1):
         for j in (0, 1):
             acc_a[2 * c + j] = jnp.abs(form(c, j, SELF, INNER_Z[j], INNER_Y[c])[2])
+            prepare(c, j)
 
     for k in (8, 9, 4, 5):
         sends[k].wait_recv()
     for c in (0, 1):
         for j in (0, 1):
-            acc_a[2 * c + j] += jnp.abs(form(c, j, OUTER_Z[j], OUTER_Y[c])[1])
+            finish(c, j, OUTER_Z[j])
+            acc_a[2 * c + j] += jnp.abs(finish(c, j, OUTER_Y[c]))
+
+    await_arrival(r0.at[4:6], z_recv.at[0])
+    below, above = r0[4, 0, 0:4], r0[5, 0, 0:4]
+    mine = m0[0, 0:4]
+    w_ref[OWN, 0:4] = jnp.where(straddle4 & even4, below, mine)
+    w_ref[ZED, 0:4] = jnp.where(even4, below, jnp.where(straddle4, mine, above))
+    apply_here()
 
     for c in (0, 1):
         sends[2 * c].wait_recv()
         sends[2 * c + 1].wait_recv()
         for j in (0, 1):
-            low, high = form(c, j, XM, XP)
-            acc_a[2 * c + j] += jnp.abs(low) + jnp.abs(high)
+            acc_a[2 * c + j] += jnp.abs(finish(c, j, XM)) + jnp.abs(finish(c, j, XP))
 
     sends[6].wait_recv()
     sends[7].wait_recv()
@@ -241,28 +291,13 @@
 
     scales = [row_sums(acc_a[t]) for t in range(4)]
 
-    pltpu.make_async_copy(r0, r0, small_recv.at[0]).wait()
-    below, above = r0[4, 0, 0:4], r0[5, 0, 0:4]
-    mine = m0[0, 0:4]
-    w_ref[OWN, 0:4] = jnp.where(straddle4 & even4, below, mine)
-    w_ref[ZED, 0:4] = jnp.where(even4, below, jnp.where(straddle4, mine, above))
-    pltpu.make_async_copy(d0, d0, far_recv).wait()
+    await_arrival(r0.at[0:4], side_recv.at[0])
+    await_arrival(d0, far_recv.at[0])
     for l in range(4):
         moved = (r0[l, 1, 0:4] > 0.5) & even4
         w_ref[2 + l, 0:4] = jnp.where(moved, d0[l, 0, 0:4], r0[l, 0, 0:4])
-
-    def apply_coarse():
-        out = []
-        for c in (0, 1):
-            for j in (0, 1):
-                t = 2 * c + j
-                acc = pieces[t, 0] * vector(c, j, 0)
-                for d in range(1, 7):
-                    acc += pieces[t, d] * vector(c, j, d)
-                out.append(row_sums(acc))
-        return out
-
-    sums = apply_coarse()
+    sums = apply_rest()
+
     rhs = rhs_ref[0, :, 0, :]
 
     def parts(c, lower, upper, extra):
@@ -283,50 +318,72 @@
         copies = [
             pltpu.make_async_remote_copy(
                 full if r < 4 else swapped, target.at[opposite(r)],
-                small_send.at[k], small_recv.at[k],
+                small_send.at[k], arrival(k, r),
                 device_id=devices[r], device_id_type=MESH,
             )
             for r in ORDER
         ]
         for copy in copies:
             copy.start()
-        pltpu.make_async_copy(target, target, small_recv.at[k]).wait()
-
-    def combined(full, target, even, straddle):
+
+    def combined_here(k, full, target, even, straddle):
+        await_arrival(target.at[4:6], z_recv.at[k])
         crossing = jnp.where(even, target[4], target[5])
-        own = full[...]
-        own = own + jnp.where(straddle, crossing, 0.0)
-        out = [own, jnp.where(straddle, own, crossing)]
+        own = full[...] + jnp.where(straddle, crossing, 0.0)
+        return [own, jnp.where(straddle, own, crossing)]
+
+    def combined_rest(k, target, even):
+        await_arrival(target.at[0:4], side_recv.at[k])
+        await_arrival(target.at[6:14], far_recv.at[k])
+        out = []
         for l in range(4):
             far = jnp.where(even, target[6 + 2 * l], target[7 + 2 * l])
             moved = r0[l, 1, 0 : even.shape[0]] > 0.5
             out.append(target[l] + jnp.where(moved, far, 0.0))
         return out
 
+    def first_step(k, total):
+        inverse = 1.0 / total[4:8]
+        inv_ref[k, 0:4] = inverse
+        w_ref[k, 0:4] = w_ref[k, 0:4] + total[0:4] * inverse
+
+    def next_step(k, total):
+        w_ref[k, 0:4] = w_ref[k, 0:4] + total * inv_ref[k, 0:4]
+
     for c in (0, 1):
         put(f1, s1, 2 * c, defects(c, sums))
         put(f1, s1, 4 + 2 * c, parts(c, scales[2 * c], scales[2 * c + 1], EPSILON))
     exchange(1, f1, s1, r1)
-    for k, total in enumerate(combined(f1, r1, even8, straddle8)):
-        inverse = 1.0 / total[4:8]
-        inv_ref[k, 0:4] = inverse
-        w_ref[k, 0:4] = w_ref[k, 0:4] + total[0:4] * inverse
-
-    sums = apply_coarse()
+    await_arrival(r0, small_send.at[0])
+    await_arrival(d0, far_send)
+    for copy in sends:
+        copy.wait_send()
+    for k, total in enumerate(combined_here(1, f1, r1, even8, straddle8)):
+        first_step(k, total)
+    apply_here()
+    for k, total in enumerate(combined_rest(1, r1, even8)):
+        first_step(2 + k, total)
+    sums = apply_rest()
+
     for c in (0, 1):
         put(f2, s2, 2 * c, defects(c, sums))
     exchange(2, f2, s2, r2)
-    for k, total in enumerate(combined(f2, r2, even4, straddle4)):
-        w_ref[k, 0:4] = w_ref[k, 0:4] + total * inv_ref[k, 0:4]
-
-    sums = apply_coarse()
+    await_arrival(r1, small_send.at[1])
+    for k, total in enumerate(combined_here(2, f2, r2, even4, straddle4)):
+        next_step(k, total)
+    apply_here()
+    for k, total in enumerate(combined_rest(2, r2, even4)):
+        next_step(2 + k, total)
+    sums = apply_rest()
+
     last = [defects(c, sums) for c in (0, 1)]
     for c in (0, 1):
         s3[c : c + 1, :] = last[c][0]
     down = pltpu.make_async_remote_copy(
-        s3, r3, small_send.at[3], small_recv.at[3], device_id=devices[4], device_id_type=MESH
+        s3, r3, small_send.at[3], last_recv, device_id=devices[4], device_id_type=MESH
     )
     down.start()
+    await_arrival(r2, small_send.at[2])
     for c in (0, 1):
         out_ref[0, c, 0:1, :] = w_ref[OWN, 2 * c + 1 : 2 * c + 2, :]
     down.wait_recv()
@@ -334,12 +391,6 @@
         out_ref[0, c, 1:2, :] = last[c][1] + jnp.where(phase[c] == 1, r3[c : c + 1, :], 0.0)
 
     down.wait_send()
-    pltpu.make_async_copy(r0, r0, small_send.at[0]).wait()
-    pltpu.make_async_copy(d0, d0, far_send).wait()
-    pltpu.make_async_copy(r1, r1, small_send.at[1]).wait()
-    pltpu.make_async_copy(r2, r2, small_send.at[2]).wait()
-    for copy in sends:
-        copy.wait_send()
 
 
 def body(a_blocks, a_cols, p_blocks, agg_ids, coarse_cols, coarse_rhs, coarse_start):
@@ -366,6 +417,8 @@
             pltpu.VMEM((2, 2, N, N), BF16),
             pltpu.VMEM((4, 7, N, N), F32),
             pltpu.VMEM((4, N, N), F32),
+            pltpu.VMEM((4, N, N), F32),
+            pltpu.VMEM((4, 4, N, 2 * N), BF16),
             pltpu.VMEM((6, 8, N), F32),
             pltpu.VMEM((2, 8, N), F32),
             pltpu.VMEM((6, 2, 8, N), F32),
@@ -385,8 +438,10 @@
             pltpu.SemaphoreType.DMA((10,)),
             pltpu.SemaphoreType.DMA((10,)),
             pltpu.SemaphoreType.DMA((4,)),
-            pltpu.SemaphoreType.DMA((4,)),
+            pltpu.SemaphoreType.DMA((3,)),
+            pltpu.SemaphoreType.DMA((3,)),
             pltpu.SemaphoreType.DMA,
+            pltpu.SemaphoreType.DMA((3,)),
             pltpu.SemaphoreType.DMA,
         ],
         compiler_params=pltpu.CompilerParams(

time: 30.9 us -> 30.8 us (level)
  no operation moved by 1% of the time
where the time goes in v5:
time: 30.8 us; the launch traced here: 30.6 us
  Pallas kernels  29.4 us (95%)
  between operations  0.64 us (2%)
  local copies, waits for them, and re-layouts  0.57 us (2%)
    pallas_call x1, Pallas kernels, body(): pl.pallas_call(kernel, out_shape=pltpu.VMEM((one, rows, 2 * layers, width...  29.4 us

profile of v5, /device:TPU:1, one launch (start us, length us, event | category | flops | bytes accessed | tf_op | source)
XLA Modules:
  0.0 30.6 jit_solution(15459149848825852574)
XLA Ops:
  0.6 29.4 %coarse_setup.1 = f32[1,2,2,128]{3,2,1,0:T(2,128)S(1)} custom-call(bf16[1,2,2,7,128,128]{5,4,3,2,1,0:T(8,128)(2,1)} %a_hbm.1, s32[1,2,2,7]{3,2,1,0:T(2,128)} %cols_hbm.1, bf16[1,2,2,128,128]{4,3,2,1,0:T(8,128)(2,1)} %p_hbm.1, s32[1,2,2]{2,1,0:T(2,128)} %agg_hbm.1, f32[1,2,1,128]{3,2,1,0:T(1,128)} %rhs_hbm.1, f32[1,2,1,128]{3,2,1,0:T(1,128)} %start_hbm.1), custom_call_target="tpu_custom_call" | custom-call | tf_op jit(solution)/shard_map/coarse_setup/pallas_call | solution.py:401
  30.1 0.6 %fusion = (f32[1,2,1,128]{3,2,1,0:T(1,128)}, f32[1,2,1,128]{3,2,1,0:T(1,128)}) fusion(f32[1,2,2,128]{3,2,1,0:T(2,128)S(1)} %coarse_setup.1), kind=kLoop, calls=%fused_computation | loop fusion | bytes 4096 | tf_op jit(solution)/shard_map/slice | solution.py:452

commit v6 on v5

--- a/solution.py
+++ b/solution.py
@@ -150,9 +150,7 @@
         )
         for r in UPWARD
     ]
-    for copy in sends[:4] + far_starts + sends[4:6] + near_starts[4:] + sends[6:]:
-        copy.start()
-    for copy in near_starts[:4]:
+    for copy in sends[:4] + far_starts + sends[4:6] + near_starts[4:] + sends[8:] + sends[6:8] + near_starts[:4]:
         copy.start()
 
     def vector(c, j, d):
@@ -234,12 +232,8 @@
             for j in (0, 1):
                 acc_y[2 * c + j] = add_up(c, j, (SELF, ZM, ZP, INNER_Y[c]))
 
-    def apply_rest():
-        return [
-            row_sums(acc_y[2 * c + j] + add_up(c, j, (OUTER_Y[c], XM, XP)))
-            for c in (0, 1)
-            for j in (0, 1)
-        ]
+    def apply_rest(c, j):
+        return row_sums(acc_y[2 * c + j] + add_up(c, j, (OUTER_Y[c], XM, XP)))
 
     for c in (0, 1):
         for j in (0, 1):
@@ -296,7 +290,7 @@
     for l in range(4):
         moved = (r0[l, 1, 0:4] > 0.5) & even4
         w_ref[2 + l, 0:4] = jnp.where(moved, d0[l, 0, 0:4], r0[l, 0, 0:4])
-    sums = apply_rest()
+    sums = [apply_rest(c, j) for c in (0, 1) for j in (0, 1)]
 
     rhs = rhs_ref[0, :, 0, :]
 
@@ -363,7 +357,7 @@
     apply_here()
     for k, total in enumerate(combined_rest(1, r1, even8)):
         first_step(2 + k, total)
-    sums = apply_rest()
+    sums = [apply_rest(c, j) for c in (0, 1) for j in (0, 1)]
 
     for c in (0, 1):
         put(f2, s2, 2 * c, defects(c, sums))
@@ -374,11 +368,9 @@
     apply_here()
     for k, total in enumerate(combined_rest(2, r2, even4)):
         next_step(2 + k, total)
-    sums = apply_rest()
-
-    last = [defects(c, sums) for c in (0, 1)]
-    for c in (0, 1):
-        s3[c : c + 1, :] = last[c][0]
+    lower = [apply_rest(c, 0) for c in (0, 1)]
+    for c in (0, 1):
+        s3[c : c + 1, :] = -lower[c]
     down = pltpu.make_async_remote_copy(
         s3, r3, small_send.at[3], last_recv, device_id=devices[4], device_id_type=MESH
     )
@@ -386,9 +378,12 @@
     await_arrival(r2, small_send.at[2])
     for c in (0, 1):
         out_ref[0, c, 0:1, :] = w_ref[OWN, 2 * c + 1 : 2 * c + 2, :]
+    upper = [apply_rest(c, 1) for c in (0, 1)]
     down.wait_recv()
     for c in (0, 1):
-        out_ref[0, c, 1:2, :] = last[c][1] + jnp.where(phase[c] == 1, r3[c : c + 1, :], 0.0)
+        out_ref[0, c, 1:2, :] = (
+            rhs[c : c + 1] - upper[c] + jnp.where(phase[c] == 1, r3[c : c + 1, :], -lower[c])
+        )
 
     down.wait_send()
 

time: 30.8 us -> 30.8 us (level)
  no operation moved by 1% of the time
where the time goes in v6:
time: 30.8 us; the launch traced here: 30.6 us
  Pallas kernels  29.4 us (95%)
  between operations  0.64 us (2%)
  local copies, waits for them, and re-layouts  0.57 us (2%)
    pallas_call x1, Pallas kernels, body(): pl.pallas_call(kernel, out_shape=pltpu.VMEM((one, rows, 2 * layers, width...  29.4 us

profile of v6, /device:TPU:1, one launch (start us, length us, event | category | flops | bytes accessed | tf_op | source)
XLA Modules:
  0.0 30.6 jit_solution(10902479000860889000)
XLA Ops:
  0.6 29.4 %coarse_setup.1 = f32[1,2,2,128]{3,2,1,0:T(2,128)S(1)} custom-call(bf16[1,2,2,7,128,128]{5,4,3,2,1,0:T(8,128)(2,1)} %a_hbm.1, s32[1,2,2,7]{3,2,1,0:T(2,128)} %cols_hbm.1, bf16[1,2,2,128,128]{4,3,2,1,0:T(8,128)(2,1)} %p_hbm.1, s32[1,2,2]{2,1,0:T(2,128)} %agg_hbm.1, f32[1,2,1,128]{3,2,1,0:T(1,128)} %rhs_hbm.1, f32[1,2,1,128]{3,2,1,0:T(1,128)} %start_hbm.1), custom_call_target="tpu_custom_call" | custom-call | tf_op jit(solution)/shard_map/coarse_setup/pallas_call | solution.py:396
  30.0 0.6 %fusion = (f32[1,2,1,128]{3,2,1,0:T(1,128)}, f32[1,2,1,128]{3,2,1,0:T(1,128)}) fusion(f32[1,2,2,128]{3,2,1,0:T(2,128)S(1)} %coarse_setup.1), kind=kLoop, calls=%fused_computation | loop fusion | bytes 4096 | tf_op jit(solution)/shard_map/slice | solution.py:447

commit v7 on v6

--- a/solution.py
+++ b/solution.py
@@ -254,14 +254,22 @@
     w_ref[ZED, 0:4] = jnp.where(even4, below, jnp.where(straddle4, mine, above))
     apply_here()
 
-    for c in (0, 1):
-        sends[2 * c].wait_recv()
-        sends[2 * c + 1].wait_recv()
+    def finish_x(c):
         for j in (0, 1):
             acc_a[2 * c + j] += jnp.abs(finish(c, j, XM)) + jnp.abs(finish(c, j, XP))
 
-    sends[6].wait_recv()
-    sends[7].wait_recv()
+    sends[0].wait_recv()
+    sends[1].wait_recv()
+    finish_x(0)
+
+    for k in (2, 3, 6, 7):
+        sends[k].wait_recv()
+    await_arrival(r0.at[0:4], side_recv.at[0])
+    await_arrival(d0, far_recv.at[0])
+    for l in range(4):
+        moved = (r0[l, 1, 0:4] > 0.5) & even4
+        w_ref[2 + l, 0:4] = jnp.where(moved, d0[l, 0, 0:4], r0[l, 0, 0:4])
+    finish_x(1)
     for c in (0, 1):
         j = 1 - c
         other = pz[1 - c, c]
@@ -285,11 +293,6 @@
 
     scales = [row_sums(acc_a[t]) for t in range(4)]
 
-    await_arrival(r0.at[0:4], side_recv.at[0])
-    await_arrival(d0, far_recv.at[0])
-    for l in range(4):
-        moved = (r0[l, 1, 0:4] > 0.5) & even4
-        w_ref[2 + l, 0:4] = jnp.where(moved, d0[l, 0, 0:4], r0[l, 0, 0:4])
     sums = [apply_rest(c, j) for c in (0, 1) for j in (0, 1)]
 
     rhs = rhs_ref[0, :, 0, :]

time: 30.8 us -> 30.5 us (level)
  no operation moved by 1% of the time
where the time goes in v7:
time: 30.5 us; the launch traced here: 30.4 us
  Pallas kernels  29.2 us (96%)
  between operations  0.64 us (2%)
  local copies, waits for them, and re-layouts  0.57 us (2%)
    pallas_call x1, Pallas kernels, body(): pl.pallas_call(kernel, out_shape=pltpu.VMEM((one, rows, 2 * layers, width...  29.2 us

profile of v7, /device:TPU:1, one launch (start us, length us, event | category | flops | bytes accessed | tf_op | source)
XLA Modules:
  0.0 30.4 jit_solution(8729778471119644342)
XLA Ops:
  0.6 29.2 %coarse_setup.1 = f32[1,2,2,128]{3,2,1,0:T(2,128)S(1)} custom-call(bf16[1,2,2,7,128,128]{5,4,3,2,1,0:T(8,128)(2,1)} %a_hbm.1, s32[1,2,2,7]{3,2,1,0:T(2,128)} %cols_hbm.1, bf16[1,2,2,128,128]{4,3,2,1,0:T(8,128)(2,1)} %p_hbm.1, s32[1,2,2]{2,1,0:T(2,128)} %agg_hbm.1, f32[1,2,1,128]{3,2,1,0:T(1,128)} %rhs_hbm.1, f32[1,2,1,128]{3,2,1,0:T(1,128)} %start_hbm.1), custom_call_target="tpu_custom_call" | custom-call | tf_op jit(solution)/shard_map/coarse_setup/pallas_call | solution.py:399
  29.8 0.6 %fusion = (f32[1,2,1,128]{3,2,1,0:T(1,128)}, f32[1,2,1,128]{3,2,1,0:T(1,128)}) fusion(f32[1,2,2,128]{3,2,1,0:T(2,128)S(1)} %coarse_setup.1), kind=kLoop, calls=%fused_computation | loop fusion | bytes 4096 | tf_op jit(solution)/shard_map/slice | solution.py:450

commit v8 on v7

--- a/solution.py
+++ b/solution.py
@@ -35,7 +35,7 @@
     cols_ref, agg_ref, rhs_ref, start_ref,
     a_v, p_v, px, py, pz, stage, partner, pieces, acc_a, acc_y, ahead,
     w_ref, m0, r0, d0, f1, s1, r1, inv_ref, f2, s2, r2, s3, r3,
-    a_sem, p_sem, in_sem, bulk_send, bulk_recv, small_send, side_recv, z_recv, far_send, far_recv, last_recv,
+    a_sem, p_sem, in_sem, bulk_send, bulk_recv, small_send, side_recv, z_recv, far_send, far_recv, far_y_recv, last_recv,
 ):
     gx, gy, gz = lax.axis_index("gx"), lax.axis_index("gy"), lax.axis_index("gz")
     nx, ny, nz = lax.axis_size("gx"), lax.axis_size("gy"), lax.axis_size("gz")
@@ -113,7 +113,9 @@
     pl.semaphore_wait(barrier, len(FACES) + len(UPWARD))
 
     def arrival(k, r):
-        return (side_recv if r < 4 else z_recv if r < 6 else far_recv).at[k]
+        return (
+            side_recv if r < 4 else z_recv if r < 6 else far_recv if r < 10 else far_y_recv
+        ).at[k]
 
     def await_arrival(buffer, semaphore):
         pltpu.make_async_copy(buffer, buffer, semaphore).wait()
@@ -232,8 +234,13 @@
             for j in (0, 1):
                 acc_y[2 * c + j] = add_up(c, j, (SELF, ZM, ZP, INNER_Y[c]))
 
-    def apply_rest(c, j):
-        return row_sums(acc_y[2 * c + j] + add_up(c, j, (OUTER_Y[c], XM, XP)))
+    def apply_y():
+        for c in (0, 1):
+            for j in (0, 1):
+                acc_y[2 * c + j] += add_up(c, j, (OUTER_Y[c],))
+
+    def apply_rest(c, j, *more):
+        return row_sums(acc_y[2 * c + j] + add_up(c, j, (*more, XM, XP)))
 
     for c in (0, 1):
         for j in (0, 1):
@@ -293,7 +300,7 @@
 
     scales = [row_sums(acc_a[t]) for t in range(4)]
 
-    sums = [apply_rest(c, j) for c in (0, 1) for j in (0, 1)]
+    sums = [apply_rest(c, j, OUTER_Y[c]) for c in (0, 1) for j in (0, 1)]
 
     rhs = rhs_ref[0, :, 0, :]
 
@@ -329,14 +336,15 @@
         own = full[...] + jnp.where(straddle, crossing, 0.0)
         return [own, jnp.where(straddle, own, crossing)]
 
-    def combined_rest(k, target, even):
-        await_arrival(target.at[0:4], side_recv.at[k])
-        await_arrival(target.at[6:14], far_recv.at[k])
+    def combined_sides(k, target, even, low):
+        await_arrival(
+            target.at[6 + 2 * low : 10 + 2 * low], (far_y_recv if low else far_recv).at[k]
+        )
         out = []
-        for l in range(4):
+        for l in (low, low + 1):
             far = jnp.where(even, target[6 + 2 * l], target[7 + 2 * l])
             moved = r0[l, 1, 0 : even.shape[0]] > 0.5
-            out.append(target[l] + jnp.where(moved, far, 0.0))
+            out.append((2 + l, target[l] + jnp.where(moved, far, 0.0)))
         return out
 
     def first_step(k, total):
@@ -358,8 +366,12 @@
     for k, total in enumerate(combined_here(1, f1, r1, even8, straddle8)):
         first_step(k, total)
     apply_here()
-    for k, total in enumerate(combined_rest(1, r1, even8)):
-        first_step(2 + k, total)
+    await_arrival(r1.at[0:4], side_recv.at[1])
+    for k, total in combined_sides(1, r1, even8, 2):
+        first_step(k, total)
+    apply_y()
+    for k, total in combined_sides(1, r1, even8, 0):
+        first_step(k, total)
     sums = [apply_rest(c, j) for c in (0, 1) for j in (0, 1)]
 
     for c in (0, 1):
@@ -369,8 +381,12 @@
     for k, total in enumerate(combined_here(2, f2, r2, even4, straddle4)):
         next_step(k, total)
     apply_here()
-    for k, total in enumerate(combined_rest(2, r2, even4)):
-        next_step(2 + k, total)
+    await_arrival(r2.at[0:4], side_recv.at[2])
+    for k, total in combined_sides(2, r2, even4, 2):
+        next_step(k, total)
+    apply_y()
+    for k, total in combined_sides(2, r2, even4, 0):
+        next_step(k, total)
     lower = [apply_rest(c, 0) for c in (0, 1)]
     for c in (0, 1):
         s3[c : c + 1, :] = -lower[c]
@@ -440,6 +456,7 @@
             pltpu.SemaphoreType.DMA((3,)),
             pltpu.SemaphoreType.DMA,
             pltpu.SemaphoreType.DMA((3,)),
+            pltpu.SemaphoreType.DMA((3,)),
             pltpu.SemaphoreType.DMA,
         ],
         compiler_params=pltpu.CompilerParams(

time: 30.5 us -> 30.6 us (level)
  no operation moved by 1% of the time
where the time goes in v8:
time: 30.6 us; the launch traced here: 30.5 us
  Pallas kernels  29.2 us (95%)
  between operations  0.64 us (2%)
  local copies, waits for them, and re-layouts  0.57 us (2%)
    pallas_call x1, Pallas kernels, body(): pl.pallas_call(kernel, out_shape=pltpu.VMEM((one, rows, 2 * layers, width...  29.2 us

profile of v8, /device:TPU:1, one launch (start us, length us, event | category | flops | bytes accessed | tf_op | source)
XLA Modules:
  0.0 30.5 jit_solution(5434937622522973176)
XLA Ops:
  0.6 29.2 %coarse_setup.1 = f32[1,2,2,128]{3,2,1,0:T(2,128)S(1)} custom-call(bf16[1,2,2,7,128,128]{5,4,3,2,1,0:T(8,128)(2,1)} %a_hbm.1, s32[1,2,2,7]{3,2,1,0:T(2,128)} %cols_hbm.1, bf16[1,2,2,128,128]{4,3,2,1,0:T(8,128)(2,1)} %p_hbm.1, s32[1,2,2]{2,1,0:T(2,128)} %agg_hbm.1, f32[1,2,1,128]{3,2,1,0:T(1,128)} %rhs_hbm.1, f32[1,2,1,128]{3,2,1,0:T(1,128)} %start_hbm.1), custom_call_target="tpu_custom_call" | custom-call | tf_op jit(solution)/shard_map/coarse_setup/pallas_call | solution.py:415
  29.9 0.6 %fusion = (f32[1,2,1,128]{3,2,1,0:T(1,128)}, f32[1,2,1,128]{3,2,1,0:T(1,128)}) fusion(f32[1,2,2,128]{3,2,1,0:T(2,128)S(1)} %coarse_setup.1), kind=kLoop, calls=%fused_computation | loop fusion | bytes 4096 | tf_op jit(solution)/shard_map/slice | solution.py:467

commit v9 on v8

--- a/solution.py
+++ b/solution.py
@@ -261,6 +261,13 @@
     w_ref[ZED, 0:4] = jnp.where(even4, below, jnp.where(straddle4, mine, above))
     apply_here()
 
+    for c in (0, 1):
+        for i in (0, 1):
+            t = 2 * c + i
+            acc_a[t] += jnp.abs(
+                jnp.where(phase[c] == 1, pieces[t, INNER_Z[i]], pieces[t, OUTER_Z[i]])
+            )
+
     def finish_x(c):
         for j in (0, 1):
             acc_a[2 * c + j] += jnp.abs(finish(c, j, XM)) + jnp.abs(finish(c, j, XP))
@@ -268,6 +275,7 @@
     sends[0].wait_recv()
     sends[1].wait_recv()
     finish_x(0)
+    first_scale = row_sums(acc_a[0])
 
     for k in (2, 3, 6, 7):
         sends[k].wait_recv()
@@ -292,13 +300,8 @@
             pieces[2 * c + 1, SELF] + pieces[2 * c + 1, ZM]
         )
         acc_a[t] += jnp.abs(jnp.where(phase[c] == 1, split, whole))
-        for i in (0, 1):
-            t = 2 * c + i
-            acc_a[t] += jnp.abs(
-                jnp.where(phase[c] == 1, pieces[t, INNER_Z[i]], pieces[t, OUTER_Z[i]])
-            )
-
-    scales = [row_sums(acc_a[t]) for t in range(4)]
+
+    scales = [first_scale] + [row_sums(acc_a[t]) for t in (1, 2, 3)]
 
     sums = [apply_rest(c, j, OUTER_Y[c]) for c in (0, 1) for j in (0, 1)]
 

time: 30.6 us -> 30.6 us (level)
  no operation moved by 1% of the time
where the time goes in v9:
time: 30.6 us; the launch traced here: 30.4 us
  Pallas kernels  29.2 us (95%)
  between operations  0.64 us (2%)
  local copies, waits for them, and re-layouts  0.57 us (2%)
    pallas_call x1, Pallas kernels, body(): pl.pallas_call(kernel, out_shape=pltpu.VMEM((one, rows, 2 * layers, width...  29.2 us

profile of v9, /device:TPU:1, one launch (start us, length us, event | category | flops | bytes accessed | tf_op | source)
XLA Modules:
  0.0 30.4 jit_solution(2934275130624540764)
XLA Ops:
  0.6 29.2 %coarse_setup.1 = f32[1,2,2,128]{3,2,1,0:T(2,128)S(1)} custom-call(bf16[1,2,2,7,128,128]{5,4,3,2,1,0:T(8,128)(2,1)} %a_hbm.1, s32[1,2,2,7]{3,2,1,0:T(2,128)} %cols_hbm.1, bf16[1,2,2,128,128]{4,3,2,1,0:T(8,128)(2,1)} %p_hbm.1, s32[1,2,2]{2,1,0:T(2,128)} %agg_hbm.1, f32[1,2,1,128]{3,2,1,0:T(1,128)} %rhs_hbm.1, f32[1,2,1,128]{3,2,1,0:T(1,128)} %start_hbm.1), custom_call_target="tpu_custom_call" | custom-call | tf_op jit(solution)/shard_map/coarse_setup/pallas_call | solution.py:418
  29.9 0.6 %fusion = (f32[1,2,1,128]{3,2,1,0:T(1,128)}, f32[1,2,1,128]{3,2,1,0:T(1,128)}) fusion(f32[1,2,2,128]{3,2,1,0:T(2,128)S(1)} %coarse_setup.1), kind=kLoop, calls=%fused_computation | loop fusion | bytes 4096 | tf_op jit(solution)/shard_map/slice | solution.py:470
